TPU v7x, 512 devices: a whole 4x4x16 slice. The times are simulated.
512 devices in a mesh: tm: 16 (over x, z_lo), space: 32 (over y, z_hi, core).
Axes of the slice: x: 4, y: 4, z: 16 (z_hi: 4, z_lo: 4; z = z_hi * 4 + z_lo), core: 2. Of those that a mesh axis runs over, the one named last changes fastest.
Arguments:
- positions: float32 [16, 3, 3, 8192], P('tm', None, None, 'space'), may hold values from -4 to 4
- velocities: float32 [16, 3, 3, 8192], P('tm', None, None, 'space'), may hold values from -3 to 3
- masses: float32 [8192], P('space'), may hold values from 0.2 to 2
- initial_places: float32 [3, 8192], P(None, 'space'), may hold values from -4 to 4
- initial_speeds: float32 [3, 8192], P(None, 'space'), may hold values from -3 to 3
Outputs:
- node_places: float32 [16, 2, 3, 8192], P('tm', None, None, 'space')
- node_speeds: float32 [16, 2, 3, 8192], P('tm', None, None, 'space')
- end_force: float32 [16, 3, 8192], P('tm', None, 'space')
- start_places: float32 [16, 3, 8192], P('tm', None, 'space')
- start_speeds: float32 [16, 3, 8192], P('tm', None, 'space')
All inputs are finite; a program needn't handle non-finite values.
Results may differ from a plain program's by a relative error of at most 0.0003.
Values sent between devices are 32-bit elements; how exact they have to be, the bound alone decides.
No kernel may reach another device: no remote copies, remote signals or barrier semaphores. Data moves between devices by JAX's collectives and lax.ppermute only.
A program may use at most 64 MiB of HBM per device.

v0:
```python
import functools

import jax
import jax.numpy as jnp
import numpy as np
from jax import lax
from jax.experimental import pallas as pl
from jax.experimental.pallas import tpu as pltpu
from jax.sharding import PartitionSpec as P

soften = 0.01
slice_length = 0.25
half_step = 0.5 * slice_length
lobatto_weights = ((5.0 / 24.0, 1.0 / 3.0, -1.0 / 24.0), (-1.0 / 24.0, 1.0 / 3.0, 5.0 / 24.0))

bodies = 8192
sources = 32
slices = 16
ring_y, ring_z, cores = 4, 4, 2
f32 = jnp.float32
bf16 = jnp.bfloat16
pull_flops = 2 * 256 * bodies * 256 * 3


def far_groups():
    places = np.arange(sources).reshape(ring_y, ring_z, cores)
    return [[int(p) for p in places[y, :, c]] for y in range(ring_y) for c in range(cores)]


def near_groups():
    places = np.arange(sources).reshape(ring_y, ring_z, cores)
    return [[int(p) for p in places[:, z, :].reshape(-1)] for z in range(ring_z)]


def product(a, b, contract):
    return lax.dot_general(a, b, (contract, ((), ())), preferred_element_type=f32)


def in_three(a):
    high = a.astype(bf16).astype(f32)
    rest = a - high
    middle = rest.astype(bf16).astype(f32)
    low = (rest - middle).astype(bf16).astype(f32)
    return high, middle, low


def own_rows(places):
    squares = jnp.sum(places * places, axis=0, keepdims=True) + soften
    high, middle, low = in_three(-2.0 * places)
    one, zero = jnp.ones_like(squares), jnp.zeros_like(squares)
    return jnp.concatenate(
        [high, high, high, middle, middle, middle, low, low, *in_three(squares), one, one, one, zero, zero], axis=0
    ).astype(bf16)


def far_rows(places):
    squares = jnp.sum(places * places, axis=0, keepdims=True)
    high, middle, low = in_three(places)
    one, zero = jnp.ones_like(squares), jnp.zeros_like(squares)
    return jnp.concatenate(
        [high, middle, low, high, middle, low, high, middle, one, one, one, *in_three(squares), zero, zero], axis=0
    ).astype(bf16)


def weight_rows(places, mass):
    weights = jnp.concatenate([places * mass, mass], axis=0)
    return jnp.concatenate([*in_three(weights), jnp.zeros_like(weights)], axis=0).astype(bf16)


def prepare(node, read, far, weight):
    def one(source, carry):
        places, mass = read(source)
        far[node, source] = far_rows(places)
        weight[node, source] = weight_rows(places, mass)
        return carry

    lax.fori_loop(0, sources, one, 0, unroll=4)


def pulls(owns, far, weight, total, unroll):
    rows = [own_rows(own) for own in owns]
    total[...] = jnp.zeros_like(total)

    def one(source, carry):
        for node in range(len(owns)):
            inverse = lax.rsqrt(product(far[node, source], rows[node], ((0,), (0,))))
            kernel = inverse * inverse * inverse
            high = kernel.astype(bf16)
            low = (kernel - high.astype(f32)).astype(bf16)
            weights = weight[node, source]
            total[node] += product(weights, high, ((1,), (0,))) + product(weights, low, ((1,), (0,)))
        return carry

    lax.fori_loop(0, sources, one, 0, unroll=unroll)
    found = []
    for node, own in enumerate(owns):
        sums = total[node]
        sums = sums[0:4] + sums[4:8] + sums[8:12]
        found.append((sums[0:3] - own * sums[3:4]) * (1.0 / bodies))
    return found


def by_node(array):
    return [jnp.concatenate([array[node, c] for c in range(3)], axis=0) for node in range(3)]


def pack_kernel(positions, velocities, masses, out):
    places, speeds = by_node(positions), by_node(velocities)
    weights = lobatto_weights[0]
    moved = slice_length * (weights[0] * speeds[0] + weights[1] * speeds[1] + weights[2] * speeds[2])
    first = places[0] + moved
    mass = masses[...]
    packed = jnp.concatenate(
        [*places, first, mass, jnp.zeros((3, mass.shape[1]), f32)], axis=0
    )
    for k in range(ring_z):
        out[k] = packed


def old_kernel(packed, own, velocities, out, state, far, weight, total):
    for node in range(3):
        prepare(
            node, lambda s, node=node: (packed[s, 3 * node : 3 * node + 3], packed[s, 12:13]), far, weight
        )
    mine = own[0]
    old = pulls([mine[3 * n : 3 * n + 3] for n in range(3)], far, weight, total, 2)
    speeds = by_node(velocities)
    kicks = [
        slice_length * (w[0] * old[0] + w[1] * old[1] + w[2] * old[2]) for w in lobatto_weights
    ]
    first_speed = speeds[0] + kicks[0]
    weights = lobatto_weights[1]
    moved = slice_length * (weights[0] * speeds[0] + weights[1] * speeds[1] + weights[2] * speeds[2])
    second = mine[9:12] + half_step * (first_speed - speeds[1]) + moved
    for k in range(sources):
        out[k] = second
    state[0] = first_speed
    state[1] = first_speed - half_step * old[1] + kicks[1]
    state[2] = second
    state[3] = second - (mine[0:3] + slice_length * speeds[0])


def middle_kernel(packed, own, velocities, state, places, speeds, drift, far, weight, total):
    prepare(0, lambda s: (packed[s, 9:12], packed[s, 12:13]), far, weight)
    mine = own[0]
    (force,) = pulls([mine[9:12]], far, weight, total, 4)
    last = state[1] + half_step * force
    for c in range(3):
        places[0, c] = jnp.concatenate([mine[9 + c : 10 + c], state[2, c : c + 1]], axis=0)
        speeds[0, c] = jnp.concatenate([state[0, c : c + 1], last[c : c + 1]], axis=0)
    both = jnp.concatenate([state[3], last - by_node(velocities)[0]], axis=0)
    for k in range(slices):
        drift[k] = both


def end_kernel(packed, places, state, out, far, weight, total):
    def read(source):
        other = (source // 8) * 8 + (source % 2) * 4 + (source // 2) % 4
        return places[source], packed[other, 12:13]

    prepare(0, read, far, weight)
    (force,) = pulls([state[2]], far, weight, total, 4)
    for c in range(3):
        out[c] = force[c : c + 1]


def start_kernel(here, drift, places, speeds, start_places, start_speeds):
    me = here[0]
    now = me.astype(f32)
    place = places[...] + (slice_length * now) * speeds[...]
    speed = speeds[...]
    for t in range(slices - 1):
        passed = jnp.where(t < me, 1.0, 0.0)
        kick = drift[t, 3:6] * passed
        place = place + drift[t, 0:3] * passed + (slice_length * (now - (t + 1.0))) * kick
        speed = speed + kick
    for c in range(3):
        start_places[c] = place[c : c + 1]
        start_speeds[c] = speed[c : c + 1]


def run(kernel, outs, scratch=(), smem=0, flops=0):
    cost = pl.CostEstimate(flops=flops, bytes_accessed=0, transcendentals=0) if flops else None

    def call(*args):
        specs = [
            pl.BlockSpec(memory_space=pltpu.SMEM if k < smem else pltpu.VMEM) for k in range(len(args))
        ]
        return pl.pallas_call(
            kernel,
            in_specs=specs,
            out_shape=outs,
            scratch_shapes=list(scratch),
            cost_estimate=cost,
            compiler_params=pltpu.CompilerParams(vmem_limit_bytes=40 * 2**20),
        )(*args)

    return call


def room(nodes):
    return (
        pltpu.VMEM((nodes, sources, 32, 256), bf16),
        pltpu.VMEM((nodes, sources, 16, 256), bf16),
        pltpu.VMEM((nodes, 16, 256), f32),
    )


def copies(array, count):
    return jnp.broadcast_to(array[None], (count, *array.shape))


def shape(*lengths):
    return jax.ShapeDtypeStruct(lengths, f32)


def body(positions, velocities, masses, initial_places, initial_speeds):
    positions = positions.transpose(1, 2, 0, 3)
    velocities = velocities.transpose(1, 2, 0, 3)
    own = run(pack_kernel, shape(ring_z, 16, 256))(positions, velocities, masses[None])
    far = lax.all_to_all(own, "space", 0, 0, axis_index_groups=far_groups(), tiled=True)
    near = copies(far.reshape(ring_z * 16, 256), ring_y * cores)
    near = lax.all_to_all(near, "space", 0, 0, axis_index_groups=near_groups(), tiled=True)
    packed = near.reshape(sources, 16, 256)
    second, state = run(old_kernel, (shape(sources, 3, 256), shape(4, 3, 256)), room(3))(packed, own, velocities)
    gathered = lax.all_to_all(second, "space", 0, 0, tiled=True)
    node_places, node_speeds, drift = run(
        middle_kernel, (shape(1, 3, 2, 256), shape(1, 3, 2, 256), shape(slices, 6, 256)), room(1), flops=pull_flops
    )(packed, own, velocities, state)
    drift, gathered = lax.optimization_barrier((drift, gathered))
    drift = lax.all_to_all(drift, "tm", 0, 0, tiled=True)
    end_force = run(end_kernel, shape(3, 1, 256), room(1), flops=pull_flops)(packed, gathered, state)
    here = lax.axis_index("tm").astype(jnp.int32)[None]
    start_places, start_speeds = run(start_kernel, (shape(3, 1, 256), shape(3, 1, 256)), smem=1)(
        here, drift, initial_places, initial_speeds
    )
    return (
        node_places.transpose(0, 2, 1, 3),
        node_speeds.transpose(0, 2, 1, 3),
        end_force.transpose(1, 0, 2),
        start_places.transpose(1, 0, 2),
        start_speeds.transpose(1, 0, 2),
    )


def solution(mesh):
    return jax.shard_map(
        body,
        mesh=mesh,
        in_specs=(
            P("tm", None, None, "space"),
            P("tm", None, None, "space"),
            P("space"),
            P(None, "space"),
            P(None, "space"),
        ),
        out_specs=(
            P("tm", None, None, "space"),
            P("tm", None, None, "space"),
            P("tm", None, "space"),
            P("tm", None, "space"),
            P("tm", None, "space"),
        ),
        check_vma=False,
    )
```

profile of v0, /device:TPU:1, one launch (start us, length us, event | category | flops | bytes accessed | tf_op | source)
XLA Modules:
  0.0 97.1 jit_solution(8954852583951187206)
XLA Ops:
  0.6 0.0 copy-start.5
  0.6 0.7 copy-done.5
  1.3 0.0 copy-start
  1.3 0.7 copy-done
  2.0 0.0 copy-start.2
  2.0 0.7 copy-done.2
  2.7 27.9 %all_to_all.20 = f32[4,16,256]{2,1,0:T(8,128)S(1)} all-to-all(f32[4,16,256]{2,1,0:T(8,128)S(1)} %shard_map.92.own), channel_id=1, replica_groups={{0,2,4,6},{1,3,5,7},{8,10,12,14},{9,11,13,15},{16,18,20,22},{17,19,21,2..., dimensions={0} | all-to-all | bytes 131072 | tf_op jit(solution)/shard_map/all_to_all | solution.py:221
  30.7 15.2 %all_to_all.21 = f32[8,64,256]{2,1,0:T(8,128)S(1)} all-to-all(f32[8,64,256]{2,1,0:T(8,128)S(1)} %broadcast_in_dim.15), channel_id=1, replica_groups={{0,1,8,9,16,17,24,25},{2,3,10,11,18,19,26,27},{4,5,12,13,20,21,28,29},{..., dimensions={0} | all-to-all | bytes 1048576 | tf_op jit(solution)/shard_map/all_to_all | solution.py:223
  45.9 14.5 %shard_map.93 = (f32[32,3,256]{2,1,0:T(4,128)}, f32[4,3,256]{2,1,0:T(4,128)S(1)}) custom-call(f32[32,16,256]{2,1,0:T(8,128)S(1)} %bitcast.11, f32[4,16,256]{2,1,0:T(8,128)S(1)} %shard_map.92.own, f32[3,3,1,256]{3,2,1,0:T(1,128)S(1)} %bitcast.15), custom_call_target="tpu_custom_call" | custom-call | tf_op jit(solution)/shard_map/pallas_call | solution.py:189
  60.4 0.0 copy-start.1
  60.4 4.7 %all-to-all-start.2 = ((f32[32,3,256]{2,1,0:T(4,128)}), f32[32,3,256]{2,1,0:T(4,128)S(1)}, u32[]{:S(2)}, u32[]{:S(2)}) async-start(f32[32,3,256]{2,1,0:T(4,128)} %get-tuple-element.18), calls=%async_computation.2 | async-start | bytes 262144 | tf_op jit(solution)/shard_map/all_to_all | solution.py:226
  65.1 0.0 copy-done.1
  65.1 6.1 %shard_map.94 = (f32[1,3,2,256]{3,2,1,0:T(2,128)}, f32[1,3,2,256]{3,2,1,0:T(2,128)}, f32[16,6,256]{2,1,0:T(8,128)}) custom-call(f32[32,16,256]{2,1,0:T(8,128)S(1)} %bitcast.12, f32[4,16,256]{2,1,0:T(8,128)S(1)} %shard_map.92.own, f32[3,3,1,256]{3,2,1,0:T(1,128)S(1)} %bitcast.16, f32[4,3,256]{2,1,0:T(4,128)S(1)} %get-tuple-element.14.state), custom_call_target="tpu_custom_call" | custom-call | flops 3221225472 | tf_op jit(solution)/shard_map/pallas_call | solution.py:189
  71.2 11.6 %all-to-all-done.2.places = f32[32,3,256]{2,1,0:T(4,128)S(1)} async-done(((f32[32,3,256]{2,1,0:T(4,128)}), f32[32,3,256]{2,1,0:T(4,128)S(1)}, u32[]{:S(2)}, u32[]{:S(2)}) %all-to-all-start.2) | async-done | bytes 98336 | tf_op jit(solution)/shard_map/all_to_all | solution.py:226
  82.8 6.4 %all-to-all-start.3 = ((f32[16,6,256]{2,1,0:T(8,128)}), f32[16,6,256]{2,1,0:T(8,128)S(1)}, u32[]{:S(2)}, u32[]{:S(2)}) async-start(f32[16,6,256]{2,1,0:T(8,128)} %get-tuple-element.20), calls=%async_computation.3 | async-start | bytes 262144 | tf_op jit(solution)/shard_map/all_to_all | solution.py:231
  89.3 0.0 copy-start.3
  89.3 0.0 copy-start.4
  89.3 6.0 %shard_map.95 = f32[3,1,256]{2,1,0:T(1,128)} custom-call(f32[32,16,256]{2,1,0:T(8,128)S(1)} %bitcast.13, f32[32,3,256]{2,1,0:T(4,128)S(1)} %all-to-all-done.2.places, f32[4,3,256]{2,1,0:T(4,128)S(1)} %get-tuple-element.14.state), custom_call_target="tpu_custom_call" | custom-call | flops 3221225472 | tf_op jit(solution)/shard_map/pallas_call | solution.py:189
  95.3 1.2 %all-to-all-done.3.drift = f32[16,6,256]{2,1,0:T(8,128)S(1)} async-done(((f32[16,6,256]{2,1,0:T(8,128)}), f32[16,6,256]{2,1,0:T(8,128)S(1)}, u32[]{:S(2)}, u32[]{:S(2)}) %all-to-all-start.3) | async-done | bytes 98336 | tf_op jit(solution)/shard_map/all_to_all | solution.py:231
  96.5 0.0 copy-done.3
  96.5 0.0 copy-done.4
  96.5 0.6 shard_map.96
  (2 shorter events, 0.1 us)
Async XLA Ops:
  0.6 0.7 copy-start.5
  1.3 0.7 copy-start
  2.0 0.7 copy-start.2
  60.4 4.7 %copy-start.1 = (f32[1,3,3,256]{3,0,2,1:T(1,128)S(1)}, f32[1,3,3,256]{3,0,2,1:T(1,128)}, u32[]{:S(2)}) copy-start(f32[1,3,3,256]{3,0,2,1:T(1,128)} %param.6) | copy-start | bytes 27652
  60.4 22.4 %all-to-all-start.2 = ((f32[32,3,256]{2,1,0:T(4,128)}), f32[32,3,256]{2,1,0:T(4,128)S(1)}, u32[]{:S(2)}, u32[]{:S(2)}) async-start(f32[32,3,256]{2,1,0:T(4,128)} %get-tuple-element.18), calls=%async_computation.2 | async-start | bytes 262144 | tf_op jit(solution)/shard_map/all_to_all | solution.py:226
  82.8 13.7 %all-to-all-start.3 = ((f32[16,6,256]{2,1,0:T(8,128)}), f32[16,6,256]{2,1,0:T(8,128)S(1)}, u32[]{:S(2)}, u32[]{:S(2)}) async-start(f32[16,6,256]{2,1,0:T(8,128)} %get-tuple-element.20), calls=%async_computation.3 | async-start | bytes 262144 | tf_op jit(solution)/shard_map/all_to_all | solution.py:231
  89.3 7.2 %copy-start.3 = (f32[3,256]{1,0:T(4,128)S(1)}, f32[3,256]{1,0:T(4,128)}, u32[]{:S(2)}) copy-start(f32[3,256]{1,0:T(4,128)} %places.1) | copy-start | bytes 9220
  89.3 7.2 %copy-start.4 = (f32[3,256]{1,0:T(4,128)S(1)}, f32[3,256]{1,0:T(4,128)}, u32[]{:S(2)}) copy-start(f32[3,256]{1,0:T(4,128)} %speeds.1) | copy-start | bytes 9220
where the time goes:
time: 97.6 us; the launch traced here: 97.1 us
  blocking collectives  43.1 us (44%)
  Pallas kernels  27.2 us (28%)
  waiting for transfers between devices  12.8 us (13%)
  starting transfers between devices  11.1 us (11%)
  local copies, waits for them, and re-layouts  2.12 us (2%)
    all_to_all x1, blocking collectives, body(): lax.all_to_all(own, 'space', 0, 0, axis_index_groups=far_groups(), tiled=...  27.9 us
    pallas_call x5, Pallas kernels, call(): pl.pallas_call(kernel, in_specs=specs, out_shape=outs, scratch_shapes=lis...  27.2 us
    all_to_all x1, blocking collectives, body(): lax.all_to_all(near, 'space', 0, 0, axis_index_groups=near_groups(), tile...  15.2 us
    all_to_all x1, waiting for transfers between devices, body(): gathered = lax.all_to_all(second, 'space', 0, 0, tiled=True)  11.6 us
    all_to_all x1, starting transfers between devices, body(): drift = lax.all_to_all(drift, 'tm', 0, 0, tiled=True)  6.43 us
    all_to_all x1, starting transfers between devices, body(): gathered = lax.all_to_all(second, 'space', 0, 0, tiled=True)  4.67 us
    unnamed x12, local copies, waits for them, and re-layouts  2.09 us
  transfers between devices with their start and end apart: 2, of which 2 were waited for; matrix products, arithmetic and copies ran while one was open for 0% of the time, Pallas kernels for 12%

commit v1 on v0

v1 whole, which is shorter than its diff:
```python
import jax
import jax.numpy as jnp
import numpy as np
from jax import lax
from jax.experimental import pallas as pl
from jax.experimental.pallas import tpu as pltpu
from jax.sharding import PartitionSpec as P

soften = 0.01
slice_length = 0.25
half_step = 0.5 * slice_length
lobatto_weights = ((5.0 / 24.0, 1.0 / 3.0, -1.0 / 24.0), (-1.0 / 24.0, 1.0 / 3.0, 5.0 / 24.0))

bodies = 8192
sources = 32
slices = 16
ring_y, ring_z, cores = 4, 4, 2
rows_sent = 13
f32 = jnp.float32
bf16 = jnp.bfloat16
pull_flops = 2 * 256 * bodies * 256 * 3


def far_groups():
    places = np.arange(sources).reshape(ring_y, ring_z, cores)
    return [[int(p) for p in places[y, :, c]] for y in range(ring_y) for c in range(cores)]


def near_groups():
    places = np.arange(sources).reshape(ring_y, ring_z, cores)
    return [[int(p) for p in places[:, z, :].reshape(-1)] for z in range(ring_z)]


def product(a, b, contract):
    return lax.dot_general(a, b, (contract, ((), ())), preferred_element_type=f32)


def in_three(a):
    high = a.astype(bf16).astype(f32)
    rest = a - high
    middle = rest.astype(bf16).astype(f32)
    low = (rest - middle).astype(bf16).astype(f32)
    return high, middle, low


def own_rows(places):
    squares = jnp.sum(places * places, axis=0, keepdims=True) + soften
    high, middle, low = in_three(-2.0 * places)
    one, zero = jnp.ones_like(squares), jnp.zeros_like(squares)
    return jnp.concatenate(
        [high, high, high, middle, middle, middle, low, low, *in_three(squares), one, one, one, zero, zero], axis=0
    ).astype(bf16)


def far_rows(places):
    squares = jnp.sum(places * places, axis=0, keepdims=True)
    high, middle, low = in_three(places)
    one, zero = jnp.ones_like(squares), jnp.zeros_like(squares)
    return jnp.concatenate(
        [high, middle, low, high, middle, low, high, middle, one, one, one, *in_three(squares), zero, zero], axis=0
    ).astype(bf16)


def weight_rows(places, mass):
    weights = jnp.concatenate([places * mass, mass], axis=0)
    return jnp.concatenate([*in_three(weights), jnp.zeros_like(weights)], axis=0).astype(bf16)


def pull_from(source, own, weight):
    inverse = lax.rsqrt(product(source, own, ((0,), (0,))))
    kernel = inverse * inverse * inverse
    high = kernel.astype(bf16)
    low = (kernel - high.astype(f32)).astype(bf16)
    return product(weight, high, ((1,), (0,))) + product(weight, low, ((1,), (0,)))


def pulls(owns, read, total, unroll):
    rows = [own_rows(own) for own in owns]
    total[...] = jnp.zeros_like(total)

    def one(near, carry):
        for far in range(ring_z):
            for node in range(len(owns)):
                places, mass = read(node, near, far)
                total[node] += pull_from(far_rows(places), rows[node], weight_rows(places, mass))
        return carry

    lax.fori_loop(0, ring_y * cores, one, 0, unroll=unroll)
    found = []
    for node, own in enumerate(owns):
        sums = total[node]
        sums = sums[0:4] + sums[4:8] + sums[8:12]
        found.append((sums[0:3] - own * sums[3:4]) * (1.0 / bodies))
    return found


def by_node(array):
    return [jnp.concatenate([array[node, c] for c in range(3)], axis=0) for node in range(3)]


def pack_kernel(positions_in, velocities_in, masses_in, out, known, positions, velocities, masses, arrived):
    pairs = ((positions_in, positions), (velocities_in, velocities), (masses_in, masses))
    moves = [pltpu.make_async_copy(a, b, arrived.at[k]) for k, (a, b) in enumerate(pairs)]
    for move in moves:
        move.start()
    for move in moves:
        move.wait()
    places, speeds = by_node(positions), by_node(velocities)
    moved = [slice_length * (w[0] * speeds[0] + w[1] * speeds[1] + w[2] * speeds[2]) for w in lobatto_weights]
    first = places[0] + moved[0]
    packed = jnp.concatenate([*places, first, masses[...]], axis=0)
    for k in range(ring_z):
        out[k] = packed
    known[0] = speeds[0]
    known[1] = first - half_step * speeds[1] + moved[1]
    known[2] = places[0] + slice_length * speeds[0]


def spread_kernel(far, out):
    for k in range(ring_y * cores):
        for z in range(ring_z):
            out[k, rows_sent * z : rows_sent * (z + 1)] = far[z]


def old_kernel(packed, own, known, out, state, total):
    def read(node, near, far):
        at = rows_sent * far
        return packed[near, at + 3 * node : at + 3 * node + 3], packed[near, at + 12 : at + 13]

    mine = own[0]
    old = pulls([mine[3 * n : 3 * n + 3] for n in range(3)], read, total, 4)
    kicks = [slice_length * (w[0] * old[0] + w[1] * old[1] + w[2] * old[2]) for w in lobatto_weights]
    first_speed = known[0] + kicks[0]
    second = known[1] + half_step * first_speed
    halves = [second[:, :128], second[:, 128:]]
    for c in range(3):
        row = jnp.concatenate([half[c : c + 1] for half in halves], axis=0)
        for k in range(sources):
            out[k, c] = row
    state[0] = first_speed
    state[1] = first_speed - half_step * old[1] + kicks[1]
    state[2] = second
    state[3] = second - known[2]


def middle_kernel(packed, own, known, state, places, speeds, drift, total):
    def read(node, near, far):
        at = rows_sent * far
        return packed[near, at + 9 : at + 12], packed[near, at + 12 : at + 13]

    mine = own[0]
    (force,) = pulls([mine[9:12]], read, total, 8)
    last = state[1] + half_step * force
    for c in range(3):
        places[0, c] = jnp.concatenate([mine[9 + c : 10 + c], state[2, c : c + 1]], axis=0)
        speeds[0, c] = jnp.concatenate([state[0, c : c + 1], last[c : c + 1]], axis=0)
    both = jnp.concatenate([state[3], last - known[0]], axis=0)
    for k in range(slices):
        drift[k] = both


def end_kernel(packed, places, state, out, total):
    def read(node, near, far):
        source = (near // cores) * (ring_z * cores) + far * cores + near % cores
        halves = [jnp.concatenate([places[source, c, h : h + 1] for c in range(3)], axis=0) for h in range(2)]
        at = rows_sent * far
        return jnp.concatenate(halves, axis=1), packed[near, at + 12 : at + 13]

    (force,) = pulls([state[2]], read, total, 8)
    for c in range(3):
        out[c] = force[c : c + 1]


def start_kernel(here, drift, places, speeds, start_places, start_speeds):
    me = here[0]
    now = me.astype(f32)
    place = places[...] + (slice_length * now) * speeds[...]
    speed = speeds[...]
    for t in range(slices - 1):
        passed = jnp.where(t < me, 1.0, 0.0)
        kick = drift[t, 3:6] * passed
        place = place + drift[t, 0:3] * passed + (slice_length * (now - (t + 1.0))) * kick
        speed = speed + kick
    for c in range(3):
        start_places[c] = place[c : c + 1]
        start_speeds[c] = speed[c : c + 1]


def run(kernel, outs, places=(), scratch=(), flops=0):
    cost = pl.CostEstimate(flops=flops, bytes_accessed=0, transcendentals=0) if flops else None

    def call(*args):
        specs = [pl.BlockSpec(memory_space=place) for place in places]
        specs += [pl.BlockSpec(memory_space=pltpu.VMEM)] * (len(args) - len(specs))
        return pl.pallas_call(
            kernel,
            in_specs=specs,
            out_shape=outs,
            scratch_shapes=list(scratch),
            cost_estimate=cost,
            compiler_params=pltpu.CompilerParams(vmem_limit_bytes=40 * 2**20),
        )(*args)

    return call


def sums(nodes):
    return (pltpu.VMEM((nodes, 16, 256), f32),)


def shape(*lengths):
    return jax.ShapeDtypeStruct(lengths, f32)


def body(positions, velocities, masses, initial_places, initial_speeds):
    positions = positions.transpose(1, 2, 0, 3)
    velocities = velocities.transpose(1, 2, 0, 3)
    masses = masses[None]
    landing = [pltpu.VMEM(a.shape, f32) for a in (positions, velocities, masses)]
    own, known = run(
        pack_kernel,
        (shape(ring_z, rows_sent, 256), shape(3, 3, 256)),
        places=(pltpu.HBM,) * 3,
        scratch=(*landing, pltpu.SemaphoreType.DMA((3,))),
    )(positions, velocities, masses)
    far = lax.all_to_all(own, "space", 0, 0, axis_index_groups=far_groups(), tiled=True)
    near = run(spread_kernel, shape(ring_y * cores, ring_z * rows_sent, 256))(far)
    packed = lax.all_to_all(near, "space", 0, 0, axis_index_groups=near_groups(), tiled=True)
    second, state = run(old_kernel, (shape(sources, 3, 2, 128), shape(4, 3, 256)), scratch=sums(3))(packed, own, known)
    gathered = lax.all_to_all(second, "space", 0, 0, tiled=True)
    node_places, node_speeds, drift = run(
        middle_kernel,
        (shape(1, 3, 2, 256), shape(1, 3, 2, 256), shape(slices, 6, 256)),
        scratch=sums(1),
        flops=pull_flops,
    )(packed, own, known, state)
    drift, gathered = lax.optimization_barrier((drift, gathered))
    drift = lax.all_to_all(drift, "tm", 0, 0, tiled=True)
    end_force = run(end_kernel, shape(3, 1, 256), scratch=sums(1), flops=pull_flops)(packed, gathered, state)
    here = lax.axis_index("tm").astype(jnp.int32)[None]
    start_places, start_speeds = run(start_kernel, (shape(3, 1, 256), shape(3, 1, 256)), places=(pltpu.SMEM,))(
        here, drift, initial_places, initial_speeds
    )
    return (
        node_places.transpose(0, 2, 1, 3),
        node_speeds.transpose(0, 2, 1, 3),
        end_force.transpose(1, 0, 2),
        start_places.transpose(1, 0, 2),
        start_speeds.transpose(1, 0, 2),
    )


def solution(mesh):
    return jax.shard_map(
        body,
        mesh=mesh,
        in_specs=(
            P("tm", None, None, "space"),
            P("tm", None, None, "space"),
            P("space"),
            P(None, "space"),
            P(None, "space"),
        ),
        out_specs=(
            P("tm", None, None, "space"),
            P("tm", None, None, "space"),
            P("tm", None, "space"),
            P("tm", None, "space"),
            P("tm", None, "space"),
        ),
        check_vma=False,
    )
```

time: 97.6 us -> 89.4 us (0.916)
  Pallas kernels: 27.2 us -> 15.2 us
  waiting for transfers between devices: 12.8 us -> 17.6 us
    pallas_call x5 -> x6, Pallas kernels: 27.2 us -> 15.2 us  [call(): pl.pallas_call(kernel, in_specs=specs, out_shape=outs, scratch_shapes=lis...]
    all_to_all x1, waiting for transfers between devices: 1.24 us -> 4.18 us  [body(): drift = lax.all_to_all(drift, 'tm', 0, 0, tiled=True)]
    all_to_all x1, waiting for transfers between devices: 11.6 us -> 13.4 us  [body(): gathered = lax.all_to_all(second, 'space', 0, 0, tiled=True)]
    unnamed x12 -> x10, local copies, waits for them, and re-layouts: 2.09 us -> 2.08 us
  transfers between devices with their start and end apart: 2 -> 2, of which waited for: 2 -> 2; matrix products, arithmetic and copies ran while one was open for 0% -> 0% of each run, Pallas kernels for 12% -> 7%
where the time goes in v1:
time: 89.4 us; the launch traced here: 88.9 us
  blocking collectives  42.5 us (48%)
  waiting for transfers between devices  17.6 us (20%)
  Pallas kernels  15.2 us (17%)
  starting transfers between devices  10.8 us (12%)
  local copies, waits for them, and re-layouts  2.08 us (2%)
    all_to_all x1, blocking collectives, body(): lax.all_to_all(own, 'space', 0, 0, axis_index_groups=far_groups(), tiled=...  27.9 us
    pallas_call x6, Pallas kernels, call(): pl.pallas_call(kernel, in_specs=specs, out_shape=outs, scratch_shapes=lis...  15.2 us
    all_to_all x1, blocking collectives, body(): lax.all_to_all(near, 'space', 0, 0, axis_index_groups=near_groups(), tile...  14.6 us
    all_to_all x1, waiting for transfers between devices, body(): gathered = lax.all_to_all(second, 'space', 0, 0, tiled=True)  13.4 us
    all_to_all x1, starting transfers between devices, body(): drift = lax.all_to_all(drift, 'tm', 0, 0, tiled=True)  6.33 us
    all_to_all x1, starting transfers between devices, body(): gathered = lax.all_to_all(second, 'space', 0, 0, tiled=True)  4.45 us
    all_to_all x1, waiting for transfers between devices, body(): drift = lax.all_to_all(drift, 'tm', 0, 0, tiled=True)  4.18 us
    unnamed x10, local copies, waits for them, and re-layouts  2.08 us
  transfers between devices with their start and end apart: 2, of which 2 were waited for; matrix products, arithmetic and copies ran while one was open for 0% of the time, Pallas kernels for 7%

profile of v1, /device:TPU:1, one launch (start us, length us, event | category | flops | bytes accessed | tf_op | source)
XLA Modules:
  0.0 88.9 jit_solution(15096438885102679390)
XLA Ops:
  0.6 0.0 copy-start.4
  0.6 0.7 copy-done.4
  1.3 0.0 copy-start
  1.3 0.7 copy-done
  2.0 0.0 copy-start.1
  2.0 0.7 copy-done.1
  2.7 0.1 shard_map.92
  2.8 27.9 %all_to_all.20.far = f32[4,13,256]{2,1,0:T(8,128)S(1)} all-to-all(f32[4,13,256]{2,1,0:T(8,128)S(1)} %get-tuple-element.16.own), channel_id=1, replica_groups={{0,2,4,6},{1,3,5,7},{8,10,12,14},{9,11,13,15},{16,18,20,22},{17,19,21,2..., dimensions={0} | all-to-all | bytes 106496 | tf_op jit(solution)/shard_map/all_to_all | solution.py:226
  30.8 14.6 %all_to_all.21.packed = f32[8,52,256]{2,1,0:T(8,128)S(1)} all-to-all(f32[8,52,256]{2,1,0:T(8,128)S(1)} %shard_map.93), channel_id=1, replica_groups={{0,1,8,9,16,17,24,25},{2,3,10,11,18,19,26,27},{4,5,12,13,20,21,28,29},{..., dimensions={0} | all-to-all | bytes 851968 | tf_op jit(solution)/shard_map/all_to_all | solution.py:228
  45.4 8.1 %shard_map.94 = (f32[32,3,2,128]{3,2,1,0:T(2,128)}, f32[4,3,256]{2,1,0:T(4,128)S(1)}) custom-call(f32[8,52,256]{2,1,0:T(8,128)S(1)} %all_to_all.21.packed, f32[4,13,256]{2,1,0:T(8,128)S(1)} %get-tuple-element.16.own, f32[3,3,256]{2,1,0:T(4,128)S(1)} %get-tuple-element.17.known), custom_call_target="tpu_custom_call" | custom-call | tf_op jit(solution)/shard_map/pallas_call | solution.py:195
  53.4 4.5 %all-to-all-start.2 = ((f32[32,3,2,128]{3,2,1,0:T(2,128)}), f32[32,3,2,128]{3,2,1,0:T(2,128)S(1)}, u32[]{:S(2)}, u32[]{:S(2)}) async-start(f32[32,3,2,128]{3,2,1,0:T(2,128)} %get-tuple-element.22), calls=%async_computation.2 | async-start | bytes 196608 | tf_op jit(solution)/shard_map/all_to_all | solution.py:230
  57.9 3.2 %shard_map.95 = (f32[1,3,2,256]{3,2,1,0:T(2,128)}, f32[1,3,2,256]{3,2,1,0:T(2,128)}, f32[16,6,256]{2,1,0:T(8,128)}) custom-call(f32[8,52,256]{2,1,0:T(8,128)S(1)} %all_to_all.21.packed, f32[4,13,256]{2,1,0:T(8,128)S(1)} %get-tuple-element.16.own, f32[3,3,256]{2,1,0:T(4,128)S(1)} %get-tuple-element.17.known, f32[4,3,256]{2,1,0:T(4,128)S(1)} %get-tuple-element.18.state), custom_call_target="tpu_custom_call" | custom-call | flops 3221225472 | tf_op jit(solution)/shard_map/pallas_call | solution.py:195
  61.1 13.4 %all-to-all-done.2.places = f32[32,3,2,128]{3,2,1,0:T(2,128)S(1)} async-done(((f32[32,3,2,128]{3,2,1,0:T(2,128)}), f32[32,3,2,128]{3,2,1,0:T(2,128)S(1)}, u32[]{:S(2)}, u32[]{:S(2)}) %all-to-all-start.2) | async-done | bytes 98336 | tf_op jit(solution)/shard_map/all_to_all | solution.py:230
  74.6 6.3 %all-to-all-start.3 = ((f32[16,6,256]{2,1,0:T(8,128)}), f32[16,6,256]{2,1,0:T(8,128)S(1)}, u32[]{:S(2)}, u32[]{:S(2)}) async-start(f32[16,6,256]{2,1,0:T(8,128)} %get-tuple-element.24), calls=%async_computation.3 | async-start | bytes 262144 | tf_op jit(solution)/shard_map/all_to_all | solution.py:238
  80.9 0.0 copy-start.2
  80.9 0.0 copy-start.3
  80.9 3.1 %shard_map.96 = f32[3,1,256]{2,1,0:T(1,128)} custom-call(f32[8,52,256]{2,1,0:T(8,128)S(1)} %all_to_all.21.packed, f32[32,3,2,128]{3,2,1,0:T(2,128)S(1)} %all-to-all-done.2.places, f32[4,3,256]{2,1,0:T(4,128)S(1)} %get-tuple-element.18.state), custom_call_target="tpu_custom_call" | custom-call | flops 3221225472 | tf_op jit(solution)/shard_map/pallas_call | solution.py:195
  84.1 4.2 %all-to-all-done.3.drift = f32[16,6,256]{2,1,0:T(8,128)S(1)} async-done(((f32[16,6,256]{2,1,0:T(8,128)}), f32[16,6,256]{2,1,0:T(8,128)S(1)}, u32[]{:S(2)}, u32[]{:S(2)}) %all-to-all-start.3) | async-done | bytes 98336 | tf_op jit(solution)/shard_map/all_to_all | solution.py:238
  88.2 0.0 copy-done.2
  88.2 0.0 copy-done.3
  88.3 0.6 shard_map.97
  (1 shorter events, 0.0 us)
Async XLA Ops:
  0.6 0.7 copy-start.4
  1.3 0.7 copy-start
  2.0 0.7 copy-start.1
  53.4 21.1 %all-to-all-start.2 = ((f32[32,3,2,128]{3,2,1,0:T(2,128)}), f32[32,3,2,128]{3,2,1,0:T(2,128)S(1)}, u32[]{:S(2)}, u32[]{:S(2)}) async-start(f32[32,3,2,128]{3,2,1,0:T(2,128)} %get-tuple-element.22), calls=%async_computation.2 | async-start | bytes 196608 | tf_op jit(solution)/shard_map/all_to_all | solution.py:230
  74.6 13.7 %all-to-all-start.3 = ((f32[16,6,256]{2,1,0:T(8,128)}), f32[16,6,256]{2,1,0:T(8,128)S(1)}, u32[]{:S(2)}, u32[]{:S(2)}) async-start(f32[16,6,256]{2,1,0:T(8,128)} %get-tuple-element.24), calls=%async_computation.3 | async-start | bytes 262144 | tf_op jit(solution)/shard_map/all_to_all | solution.py:238
  80.9 7.4 %copy-start.2 = (f32[3,256]{1,0:T(4,128)S(1)}, f32[3,256]{1,0:T(4,128)}, u32[]{:S(2)}) copy-start(f32[3,256]{1,0:T(4,128)} %places.1) | copy-start | bytes 9220
  80.9 7.3 %copy-start.3 = (f32[3,256]{1,0:T(4,128)S(1)}, f32[3,256]{1,0:T(4,128)}, u32[]{:S(2)}) copy-start(f32[3,256]{1,0:T(4,128)} %speeds.1) | copy-start | bytes 9220

commit v2 on v1

--- a/solution.py
+++ b/solution.py
@@ -15,6 +15,7 @@
 sources = 32
 slices = 16
 ring_y, ring_z, cores = 4, 4, 2
+line = 4
 rows_sent = 13
 f32 = jnp.float32
 bf16 = jnp.bfloat16
@@ -29,6 +30,10 @@
 def near_groups():
     places = np.arange(sources).reshape(ring_y, ring_z, cores)
     return [[int(p) for p in places[:, z, :].reshape(-1)] for z in range(ring_z)]
+
+
+def line_groups():
+    return [[x * line + k for k in range(line)] for x in range(slices // line)]
 
 
 def product(a, b, contract):
@@ -143,7 +148,7 @@
     state[3] = second - known[2]
 
 
-def middle_kernel(packed, own, known, state, places, speeds, drift, total):
+def middle_kernel(here, packed, own, known, state, places, speeds, drift, total):
     def read(node, near, far):
         at = rows_sent * far
         return packed[near, at + 9 : at + 12], packed[near, at + 12 : at + 13]
@@ -154,9 +159,22 @@
     for c in range(3):
         places[0, c] = jnp.concatenate([mine[9 + c : 10 + c], state[2, c : c + 1]], axis=0)
         speeds[0, c] = jnp.concatenate([state[0, c : c + 1], last[c : c + 1]], axis=0)
-    both = jnp.concatenate([state[3], last - known[0]], axis=0)
-    for k in range(slices):
-        drift[k] = both
+    kick = last - known[0]
+    drift[0:3] = state[3] - (slice_length * here[0].astype(f32)) * kick
+    drift[3:6] = kick
+
+
+def pair_kernel(here, drift, other, pair, earlier):
+    got = other[...]
+    pair[...] = drift[...] + got
+    earlier[...] = got * jnp.where((here[0] // line) % 2 == 1, 1.0, 0.0)
+
+
+def four_kernel(here, drift, earlier, other, out):
+    passed = earlier[...] + other[...] * jnp.where(here[0] // line >= 2, 1.0, 0.0)
+    for k in range(line):
+        out[k, 0:6] = passed
+        out[k, 6:12] = drift[...]
 
 
 def end_kernel(packed, places, state, out, total):
@@ -172,21 +190,20 @@
 
 
 def start_kernel(here, drift, places, speeds, start_places, start_speeds):
-    me = here[0]
-    now = me.astype(f32)
-    place = places[...] + (slice_length * now) * speeds[...]
-    speed = speeds[...]
-    for t in range(slices - 1):
-        passed = jnp.where(t < me, 1.0, 0.0)
-        kick = drift[t, 3:6] * passed
-        place = place + drift[t, 0:3] * passed + (slice_length * (now - (t + 1.0))) * kick
-        speed = speed + kick
+    now = here[0].astype(f32)
+    mine = here[0] % line
+    passed = jnp.zeros((6, drift.shape[2]), f32)
+    for k in range(line):
+        passed = passed + drift[k, 0:6] + drift[k, 6:12] * jnp.where(k < mine, 1.0, 0.0)
+    kick = passed[3:6]
+    place = places[...] + (slice_length * now) * speeds[...] + passed[0:3] + (slice_length * (now - 1.0)) * kick
+    speed = speeds[...] + kick
     for c in range(3):
         start_places[c] = place[c : c + 1]
         start_speeds[c] = speed[c : c + 1]
 
 
-def run(kernel, outs, places=(), scratch=(), flops=0):
+def run(kernel, outs, places=(), scratch=(), flops=0, room=40):
     cost = pl.CostEstimate(flops=flops, bytes_accessed=0, transcendentals=0) if flops else None
 
     def call(*args):
@@ -198,7 +215,7 @@
             out_shape=outs,
             scratch_shapes=list(scratch),
             cost_estimate=cost,
-            compiler_params=pltpu.CompilerParams(vmem_limit_bytes=40 * 2**20),
+            compiler_params=pltpu.CompilerParams(vmem_limit_bytes=room * 2**20),
         )(*args)
 
     return call
@@ -222,22 +239,28 @@
         (shape(ring_z, rows_sent, 256), shape(3, 3, 256)),
         places=(pltpu.HBM,) * 3,
         scratch=(*landing, pltpu.SemaphoreType.DMA((3,))),
+        room=60,
     )(positions, velocities, masses)
     far = lax.all_to_all(own, "space", 0, 0, axis_index_groups=far_groups(), tiled=True)
     near = run(spread_kernel, shape(ring_y * cores, ring_z * rows_sent, 256))(far)
     packed = lax.all_to_all(near, "space", 0, 0, axis_index_groups=near_groups(), tiled=True)
     second, state = run(old_kernel, (shape(sources, 3, 2, 128), shape(4, 3, 256)), scratch=sums(3))(packed, own, known)
     gathered = lax.all_to_all(second, "space", 0, 0, tiled=True)
+    here = lax.axis_index("tm").astype(jnp.int32)[None]
     node_places, node_speeds, drift = run(
         middle_kernel,
-        (shape(1, 3, 2, 256), shape(1, 3, 2, 256), shape(slices, 6, 256)),
+        (shape(1, 3, 2, 256), shape(1, 3, 2, 256), shape(6, 256)),
+        places=(pltpu.SMEM,),
         scratch=sums(1),
         flops=pull_flops,
-    )(packed, own, known, state)
+    )(here, packed, own, known, state)
+    other = lax.ppermute(drift, "tm", [(t, t ^ line) for t in range(slices)])
+    pair, earlier = run(pair_kernel, (shape(6, 256), shape(6, 256)), places=(pltpu.SMEM,))(here, drift, other)
+    other = lax.ppermute(pair, "tm", [(t, t ^ (2 * line)) for t in range(slices)])
+    drift = run(four_kernel, shape(line, 12, 256), places=(pltpu.SMEM,))(here, drift, earlier, other)
     drift, gathered = lax.optimization_barrier((drift, gathered))
-    drift = lax.all_to_all(drift, "tm", 0, 0, tiled=True)
+    drift = lax.all_to_all(drift, "tm", 0, 0, axis_index_groups=line_groups(), tiled=True)
     end_force = run(end_kernel, shape(3, 1, 256), scratch=sums(1), flops=pull_flops)(packed, gathered, state)
-    here = lax.axis_index("tm").astype(jnp.int32)[None]
     start_places, start_speeds = run(start_kernel, (shape(3, 1, 256), shape(3, 1, 256)), places=(pltpu.SMEM,))(
         here, drift, initial_places, initial_speeds
     )

time: 89.4 us -> 84.2 us (0.942)
  waiting for transfers between devices: 17.6 us -> 6.56 us
  starting transfers between devices: 10.8 us -> 16 us
  local copies, waits for them, and re-layouts: 2.08 us -> 0.02 us
  Pallas kernels: 15.2 us -> 17 us
    all_to_all x1, waiting for transfers between devices: 13.4 us -> 2.01 us  [body(): gathered = lax.all_to_all(second, 'space', 0, 0, tiled=True)]
    ppermute x0 -> x2, starting transfers between devices: none -> 7.75 us  [the longest x1 4.64 us: body(): other = lax.ppermute(pair, 'tm', [(t, t ^ 2 * line) for t in range(slices)])]
    ppermute x0 -> x2, waiting for transfers between devices: none -> 3.09 us  [the longest x1 1.56 us: body(): other = lax.ppermute(drift, 'tm', [(t, t ^ line) for t in range(slices)])]
    all_to_all x1, waiting for transfers between devices: 4.18 us -> 1.45 us  [body(): lax.all_to_all(drift, 'tm', 0, 0, axis_index_groups=line_groups(), tiled=...]
    all_to_all x1, starting transfers between devices: 6.33 us -> 3.76 us  [body(): lax.all_to_all(drift, 'tm', 0, 0, axis_index_groups=line_groups(), tiled=...]
    unnamed x10 -> x8, local copies, waits for them, and re-layouts: 2.08 us -> 0.02 us
    pallas_call x6 -> x8, Pallas kernels: 15.2 us -> 17 us  [call(): pl.pallas_call(kernel, in_specs=specs, out_shape=outs, scratch_shapes=lis...]
  transfers between devices with their start and end apart: 2 -> 4, of which waited for: 2 -> 4; matrix products, arithmetic and copies ran while one was open for 0% -> 0% of each run, Pallas kernels for 7% -> 8%
where the time goes in v2:
time: 84.2 us; the launch traced here: 83.1 us
  blocking collectives  42.9 us (51%)
  Pallas kernels  17 us (20%)
  starting transfers between devices  16 us (19%)
  waiting for transfers between devices  6.56 us (8%)
    all_to_all x1, blocking collectives, body(): lax.all_to_all(own, 'space', 0, 0, axis_index_groups=far_groups(), tiled=...  28.1 us
    pallas_call x8, Pallas kernels, call(): pl.pallas_call(kernel, in_specs=specs, out_shape=outs, scratch_shapes=lis...  17 us
    all_to_all x1, blocking collectives, body(): lax.all_to_all(near, 'space', 0, 0, axis_index_groups=near_groups(), tile...  14.7 us
    ppermute x1, starting transfers between devices, body(): other = lax.ppermute(pair, 'tm', [(t, t ^ 2 * line) for t in range(slices)])  4.64 us
    all_to_all x1, starting transfers between devices, body(): gathered = lax.all_to_all(second, 'space', 0, 0, tiled=True)  4.46 us
    all_to_all x1, starting transfers between devices, body(): lax.all_to_all(drift, 'tm', 0, 0, axis_index_groups=line_groups(), tiled=...  3.76 us
    ppermute x1, starting transfers between devices, body(): other = lax.ppermute(drift, 'tm', [(t, t ^ line) for t in range(slices)])  3.11 us
    all_to_all x1, waiting for transfers between devices, body(): gathered = lax.all_to_all(second, 'space', 0, 0, tiled=True)  2.01 us
  transfers between devices with their start and end apart: 4, of which 4 were waited for; matrix products, arithmetic and copies ran while one was open for 0% of the time, Pallas kernels for 8%

profile of v2, /device:TPU:1, one launch (start us, length us, event | category | flops | bytes accessed | tf_op | source)
XLA Modules:
  0.0 83.1 jit_solution(14735791876152438245)
XLA Ops:
  0.6 1.4 %shard_map.92 = (f32[4,13,256]{2,1,0:T(8,128)}, f32[3,3,256]{2,1,0:T(4,128)}) custom-call(f32[3,3,1,256]{3,2,1,0:T(1,128)} %bitcast.9, f32[3,3,1,256]{3,2,1,0:T(1,128)} %bitcast.10, f32[1,256]{1,0:T(1,128)} %bitcast.11), custom_call_target="tpu_custom_call" | custom-call | tf_op jit(solution)/shard_map/pallas_call | solution.py:212
  2.0 28.1 %all_to_all.20.far = f32[4,13,256]{2,1,0:T(8,128)S(1)} all-to-all(f32[4,13,256]{2,1,0:T(8,128)} %get-tuple-element.18.own), channel_id=1, replica_groups={{0,2,4,6},{1,3,5,7},{8,10,12,14},{9,11,13,15},{16,18,20,22},{17,19,21,2..., dimensions={0} | all-to-all | bytes 106496 | tf_op jit(solution)/shard_map/all_to_all | solution.py:244
  30.2 0.0 copy-start
  30.2 0.0 copy-start.1
  30.2 14.7 %all_to_all.21.packed = f32[8,52,256]{2,1,0:T(8,128)S(1)} all-to-all(f32[8,52,256]{2,1,0:T(8,128)S(1)} %shard_map.93), channel_id=1, replica_groups={{0,1,8,9,16,17,24,25},{2,3,10,11,18,19,26,27},{4,5,12,13,20,21,28,29},{..., dimensions={0} | all-to-all | bytes 851968 | tf_op jit(solution)/shard_map/all_to_all | solution.py:246
  45.0 0.0 copy-done
  45.0 0.0 copy-done.1
  45.0 8.0 %shard_map.94 = (f32[32,3,2,128]{3,2,1,0:T(2,128)}, f32[4,3,256]{2,1,0:T(4,128)S(1)}) custom-call(f32[8,52,256]{2,1,0:T(8,128)S(1)} %all_to_all.21.packed, f32[4,13,256]{2,1,0:T(8,128)S(1)} %copy-done, f32[3,3,256]{2,1,0:T(4,128)S(1)} %copy-done.1), custom_call_target="tpu_custom_call" | custom-call | tf_op jit(solution)/shard_map/pallas_call | solution.py:212
  53.0 4.5 %all-to-all-start.2 = ((f32[32,3,2,128]{3,2,1,0:T(2,128)}), f32[32,3,2,128]{3,2,1,0:T(2,128)S(1)}, u32[]{:S(2)}, u32[]{:S(2)}) async-start(f32[32,3,2,128]{3,2,1,0:T(2,128)} %get-tuple-element.26), calls=%async_computation.2 | async-start | bytes 196608 | tf_op jit(solution)/shard_map/all_to_all | solution.py:248
  57.5 3.2 %shard_map.95 = (f32[1,3,2,256]{3,2,1,0:T(2,128)}, f32[1,3,2,256]{3,2,1,0:T(2,128)}, f32[6,256]{1,0:T(8,128)S(1)}) custom-call(s32[1]{0:T(128)} %bitcast.here, f32[8,52,256]{2,1,0:T(8,128)S(1)} %all_to_all.21.packed, f32[4,13,256]{2,1,0:T(8,128)S(1)} %copy-done, f32[3,3,256]{2,1,0:T(4,128)S(1)} %copy-done.1, f32[4,3,256]{2,1,0:T(4,128)S(1)} %get-tuple-element.20.state), custom_call_target="tpu_custom_call" | custom-call | flops 3221225472 | tf_op jit(solution)/shard_map/pallas_call | solution.py:212
  60.7 3.1 %collective-permute-start = (f32[6,256]{1,0:T(8,128)S(1)}, f32[6,256]{1,0:T(8,128)S(1)}, u32[]{:S(2)}, u32[]{:S(2)}) collective-permute-start(f32[6,256]{1,0:T(8,128)S(1)} %get-tuple-element.23.drift), channel_id=1, source_target_pairs={{0,128},{32,160},{64,192},{96,224},{128,0},{160,32},{192,64},{224,... | collective-permute-start | bytes 18440 | tf_op jit(solution)/shard_map/ppermute | solution.py:257
  63.8 1.6 %collective-permute-done.other = f32[6,256]{1,0:T(8,128)S(1)} collective-permute-done((f32[6,256]{1,0:T(8,128)S(1)}, f32[6,256]{1,0:T(8,128)S(1)}, u32[]{:S(2)}, u32[]{:S(2)}) %collective-permute-start) | collective-permute-done | bytes 6176 | tf_op jit(solution)/shard_map/ppermute | solution.py:257
  65.3 4.6 %collective-permute-start.1 = (f32[6,256]{1,0:T(8,128)S(1)}, f32[6,256]{1,0:T(8,128)S(1)}, u32[]{:S(2)}, u32[]{:S(2)}) collective-permute-start(f32[6,256]{1,0:T(8,128)S(1)} %get-tuple-element.25), channel_id=1, source_target_pairs={{0,256},{32,288},{64,320},{96,352},{128,384},{160,416},{192,448},{... | collective-permute-start | bytes 18440 | tf_op jit(solution)/shard_map/ppermute | solution.py:259
  70.0 1.5 %collective-permute-done.1.other = f32[6,256]{1,0:T(8,128)S(1)} collective-permute-done((f32[6,256]{1,0:T(8,128)S(1)}, f32[6,256]{1,0:T(8,128)S(1)}, u32[]{:S(2)}, u32[]{:S(2)}) %collective-permute-start.1) | collective-permute-done | bytes 6176 | tf_op jit(solution)/shard_map/ppermute | solution.py:259
  71.5 0.6 shard_map.97
  72.1 2.0 %all-to-all-done.2.places = f32[32,3,2,128]{3,2,1,0:T(2,128)S(1)} async-done(((f32[32,3,2,128]{3,2,1,0:T(2,128)}), f32[32,3,2,128]{3,2,1,0:T(2,128)S(1)}, u32[]{:S(2)}, u32[]{:S(2)}) %all-to-all-start.2) | async-done | bytes 98336 | tf_op jit(solution)/shard_map/all_to_all | solution.py:248
  74.2 3.8 %all-to-all-start.3 = ((f32[4,12,256]{2,1,0:T(8,128)}), f32[4,12,256]{2,1,0:T(8,128)S(1)}, u32[]{:S(2)}, u32[]{:S(2)}) async-start(f32[4,12,256]{2,1,0:T(8,128)} %shard_map.97), calls=%async_computation.3 | async-start | bytes 131072 | tf_op jit(solution)/shard_map/all_to_all | solution.py:262
  77.9 0.0 copy-start.2
  77.9 0.0 copy-start.3
  77.9 3.1 %shard_map.98 = f32[3,1,256]{2,1,0:T(1,128)} custom-call(f32[8,52,256]{2,1,0:T(8,128)S(1)} %all_to_all.21.packed, f32[32,3,2,128]{3,2,1,0:T(2,128)S(1)} %all-to-all-done.2.places, f32[4,3,256]{2,1,0:T(4,128)S(1)} %get-tuple-element.20.state), custom_call_target="tpu_custom_call" | custom-call | flops 3221225472 | tf_op jit(solution)/shard_map/pallas_call | solution.py:212
  81.1 1.4 %all-to-all-done.3.drift = f32[4,12,256]{2,1,0:T(8,128)S(1)} async-done(((f32[4,12,256]{2,1,0:T(8,128)}), f32[4,12,256]{2,1,0:T(8,128)S(1)}, u32[]{:S(2)}, u32[]{:S(2)}) %all-to-all-start.3) | async-done | bytes 49184 | tf_op jit(solution)/shard_map/all_to_all | solution.py:262
  82.5 0.0 copy-done.2
  82.5 0.0 copy-done.3
  82.5 0.6 shard_map.99
  (2 shorter events, 0.0 us)
Async XLA Ops:
  30.2 14.8 %copy-start = (f32[4,13,256]{2,1,0:T(8,128)S(1)}, f32[4,13,256]{2,1,0:T(8,128)}, u32[]{:S(2)}) copy-start(f32[4,13,256]{2,1,0:T(8,128)} %get-tuple-element.18.own) | copy-start | bytes 159748
  30.2 14.7 %copy-start.1 = (f32[3,3,256]{2,1,0:T(4,128)S(1)}, f32[3,3,256]{2,1,0:T(4,128)}, u32[]{:S(2)}) copy-start(f32[3,3,256]{2,1,0:T(4,128)} %get-tuple-element.19.known) | copy-start | bytes 27652
  53.0 21.1 %all-to-all-start.2 = ((f32[32,3,2,128]{3,2,1,0:T(2,128)}), f32[32,3,2,128]{3,2,1,0:T(2,128)S(1)}, u32[]{:S(2)}, u32[]{:S(2)}) async-start(f32[32,3,2,128]{3,2,1,0:T(2,128)} %get-tuple-element.26), calls=%async_computation.2 | async-start | bytes 196608 | tf_op jit(solution)/shard_map/all_to_all | solution.py:248
  60.7 4.7 %collective-permute-start = (f32[6,256]{1,0:T(8,128)S(1)}, f32[6,256]{1,0:T(8,128)S(1)}, u32[]{:S(2)}, u32[]{:S(2)}) collective-permute-start(f32[6,256]{1,0:T(8,128)S(1)} %get-tuple-element.23.drift), channel_id=1, source_target_pairs={{0,128},{32,160},{64,192},{96,224},{128,0},{160,32},{192,64},{224,... | collective-permute-start | bytes 18440 | tf_op jit(solution)/shard_map/ppermute | solution.py:257
  65.3 6.2 %collective-permute-start.1 = (f32[6,256]{1,0:T(8,128)S(1)}, f32[6,256]{1,0:T(8,128)S(1)}, u32[]{:S(2)}, u32[]{:S(2)}) collective-permute-start(f32[6,256]{1,0:T(8,128)S(1)} %get-tuple-element.25), channel_id=1, source_target_pairs={{0,256},{32,288},{64,320},{96,352},{128,384},{160,416},{192,448},{... | collective-permute-start | bytes 18440 | tf_op jit(solution)/shard_map/ppermute | solution.py:259
  74.2 8.4 %all-to-all-start.3 = ((f32[4,12,256]{2,1,0:T(8,128)}), f32[4,12,256]{2,1,0:T(8,128)S(1)}, u32[]{:S(2)}, u32[]{:S(2)}) async-start(f32[4,12,256]{2,1,0:T(8,128)} %shard_map.97), calls=%async_computation.3 | async-start | bytes 131072 | tf_op jit(solution)/shard_map/all_to_all | solution.py:262
  77.9 4.6 %copy-start.2 = (f32[3,256]{1,0:T(4,128)S(1)}, f32[3,256]{1,0:T(4,128)}, u32[]{:S(2)}) copy-start(f32[3,256]{1,0:T(4,128)} %places.1) | copy-start | bytes 9220
  77.9 4.6 %copy-start.3 = (f32[3,256]{1,0:T(4,128)S(1)}, f32[3,256]{1,0:T(4,128)}, u32[]{:S(2)}) copy-start(f32[3,256]{1,0:T(4,128)} %speeds.1) | copy-start | bytes 9220

commit v3 on v2

--- a/solution.py
+++ b/solution.py
@@ -79,24 +79,32 @@
     return product(weight, high, ((1,), (0,))) + product(weight, low, ((1,), (0,)))
 
 
-def pulls(owns, read, total, unroll):
+def add_pulls(owns, read, blocks, total):
     rows = [own_rows(own) for own in owns]
-    total[...] = jnp.zeros_like(total)
-
-    def one(near, carry):
+
+    def one(block, carry):
         for far in range(ring_z):
             for node in range(len(owns)):
-                places, mass = read(node, near, far)
+                places, mass = read(node, block, far)
                 total[node] += pull_from(far_rows(places), rows[node], weight_rows(places, mass))
         return carry
 
-    lax.fori_loop(0, ring_y * cores, one, 0, unroll=unroll)
+    lax.fori_loop(0, blocks, one, 0, unroll=blocks)
+
+
+def forces(owns, total):
     found = []
     for node, own in enumerate(owns):
         sums = total[node]
         sums = sums[0:4] + sums[4:8] + sums[8:12]
         found.append((sums[0:3] - own * sums[3:4]) * (1.0 / bodies))
     return found
+
+
+def pulls(owns, read, total):
+    total[...] = jnp.zeros_like(total)
+    add_pulls(owns, read, ring_y * cores, total)
+    return forces(owns, total)
 
 
 def by_node(array):
@@ -127,13 +135,28 @@
             out[k, rows_sent * z : rows_sent * (z + 1)] = far[z]
 
 
-def old_kernel(packed, own, known, out, state, total):
-    def read(node, near, far):
+def nodes_of(mine):
+    return [mine[3 * n : 3 * n + 3] for n in range(3)]
+
+
+def column_kernel(far, own, total):
+    def read(node, block, z):
+        return far[z, 3 * node : 3 * node + 3], far[z, 12:13]
+
+    total[...] = jnp.zeros_like(total)
+    add_pulls(nodes_of(own[0]), read, 1, total)
+
+
+def old_kernel(here, packed, own, known, column, out, state, total):
+    def read(node, block, far):
+        near = (here[0] + block + 1) % (ring_y * cores)
         at = rows_sent * far
         return packed[near, at + 3 * node : at + 3 * node + 3], packed[near, at + 12 : at + 13]
 
-    mine = own[0]
-    old = pulls([mine[3 * n : 3 * n + 3] for n in range(3)], read, total, 4)
+    total[...] = column[...]
+    owns = nodes_of(own[0])
+    add_pulls(owns, read, ring_y * cores - 1, total)
+    old = forces(owns, total)
     kicks = [slice_length * (w[0] * old[0] + w[1] * old[1] + w[2] * old[2]) for w in lobatto_weights]
     first_speed = known[0] + kicks[0]
     second = known[1] + half_step * first_speed
@@ -154,7 +177,7 @@
         return packed[near, at + 9 : at + 12], packed[near, at + 12 : at + 13]
 
     mine = own[0]
-    (force,) = pulls([mine[9:12]], read, total, 8)
+    (force,) = pulls([mine[9:12]], read, total)
     last = state[1] + half_step * force
     for c in range(3):
         places[0, c] = jnp.concatenate([mine[9 + c : 10 + c], state[2, c : c + 1]], axis=0)
@@ -184,7 +207,7 @@
         at = rows_sent * far
         return jnp.concatenate(halves, axis=1), packed[near, at + 12 : at + 13]
 
-    (force,) = pulls([state[2]], read, total, 8)
+    (force,) = pulls([state[2]], read, total)
     for c in range(3):
         out[c] = force[c : c + 1]
 
@@ -244,7 +267,12 @@
     far = lax.all_to_all(own, "space", 0, 0, axis_index_groups=far_groups(), tiled=True)
     near = run(spread_kernel, shape(ring_y * cores, ring_z * rows_sent, 256))(far)
     packed = lax.all_to_all(near, "space", 0, 0, axis_index_groups=near_groups(), tiled=True)
-    second, state = run(old_kernel, (shape(sources, 3, 2, 128), shape(4, 3, 256)), scratch=sums(3))(packed, own, known)
+    column = run(column_kernel, shape(3, 16, 256), flops=pull_flops)(far, own)
+    place = lax.axis_index("space").astype(jnp.int32)
+    place = ((place // (ring_z * cores)) * cores + place % cores)[None]
+    second, state = run(
+        old_kernel, (shape(sources, 3, 2, 128), shape(4, 3, 256)), places=(pltpu.SMEM,), scratch=sums(3)
+    )(place, packed, own, known, column)
     gathered = lax.all_to_all(second, "space", 0, 0, tiled=True)
     here = lax.axis_index("tm").astype(jnp.int32)[None]
     node_places, node_speeds, drift = run(

time: 84.2 us -> 83.9 us (level)
  blocking collectives: 42.9 us -> 28.1 us
  waiting for transfers between devices: 6.56 us -> 14.2 us
  starting transfers between devices: 16 us -> 22.1 us
    all_to_all x1 -> x0, blocking collectives: 14.7 us -> none  [body(): lax.all_to_all(near, 'space', 0, 0, axis_index_groups=near_groups(), tile...]
    all_to_all x0 -> x1, waiting for transfers between devices: none -> 7.61 us  [body(): lax.all_to_all(near, 'space', 0, 0, axis_index_groups=near_groups(), tile...]
    all_to_all x0 -> x1, starting transfers between devices: none -> 6.19 us  [body(): lax.all_to_all(near, 'space', 0, 0, axis_index_groups=near_groups(), tile...]
    pallas_call x8 -> x9, Pallas kernels: 17 us -> 17.8 us  [call(): pl.pallas_call(kernel, in_specs=specs, out_shape=outs, scratch_shapes=lis...]
  transfers between devices with their start and end apart: 4 -> 5, of which waited for: 4 -> 5; matrix products, arithmetic and copies ran while one was open for 0% -> 0% of each run, Pallas kernels for 8% -> 10%
where the time goes in v3:
time: 83.9 us; the launch traced here: 82.8 us
  blocking collectives  28.1 us (33%)
  starting transfers between devices  22.1 us (26%)
  Pallas kernels  17.8 us (21%)
  waiting for transfers between devices  14.2 us (17%)
    all_to_all x1, blocking collectives, body(): lax.all_to_all(own, 'space', 0, 0, axis_index_groups=far_groups(), tiled=...  28.1 us
    pallas_call x9, Pallas kernels, call(): pl.pallas_call(kernel, in_specs=specs, out_shape=outs, scratch_shapes=lis...  17.8 us
    all_to_all x1, waiting for transfers between devices, body(): lax.all_to_all(near, 'space', 0, 0, axis_index_groups=near_groups(), tile...  7.61 us
    all_to_all x1, starting transfers between devices, body(): lax.all_to_all(near, 'space', 0, 0, axis_index_groups=near_groups(), tile...  6.19 us
    ppermute x1, starting transfers between devices, body(): other = lax.ppermute(pair, 'tm', [(t, t ^ 2 * line) for t in range(slices)])  4.64 us
    all_to_all x1, starting transfers between devices, body(): gathered = lax.all_to_all(second, 'space', 0, 0, tiled=True)  4.37 us
    all_to_all x1, starting transfers between devices, body(): lax.all_to_all(drift, 'tm', 0, 0, axis_index_groups=line_groups(), tiled=...  3.76 us
    ppermute x1, starting transfers between devices, body(): other = lax.ppermute(drift, 'tm', [(t, t ^ line) for t in range(slices)])  3.11 us
  transfers between devices with their start and end apart: 5, of which 5 were waited for; matrix products, arithmetic and copies ran while one was open for 0% of the time, Pallas kernels for 10%

profile of v3, /device:TPU:1, one launch (start us, length us, event | category | flops | bytes accessed | tf_op | source)
XLA Modules:
  0.0 82.8 jit_solution(11896506563992293822)
XLA Ops:
  0.6 1.4 %shard_map.92 = (f32[4,13,256]{2,1,0:T(8,128)}, f32[3,3,256]{2,1,0:T(4,128)}) custom-call(f32[3,3,1,256]{3,2,1,0:T(1,128)} %bitcast.10, f32[3,3,1,256]{3,2,1,0:T(1,128)} %bitcast.11, f32[1,256]{1,0:T(1,128)} %bitcast.12), custom_call_target="tpu_custom_call" | custom-call | tf_op jit(solution)/shard_map/pallas_call | solution.py:235
  2.0 28.1 %all_to_all.20.far = f32[4,13,256]{2,1,0:T(8,128)S(1)} all-to-all(f32[4,13,256]{2,1,0:T(8,128)} %get-tuple-element.18.own), channel_id=1, replica_groups={{0,2,4,6},{1,3,5,7},{8,10,12,14},{9,11,13,15},{16,18,20,22},{17,19,21,2..., dimensions={0} | all-to-all | bytes 106496 | tf_op jit(solution)/shard_map/all_to_all | solution.py:267
  30.2 0.8 shard_map.93
  31.0 0.0 copy-start
  31.0 6.2 %all-to-all-start.1 = ((f32[8,52,256]{2,1,0:T(8,128)}), f32[8,52,256]{2,1,0:T(8,128)S(1)}, u32[]{:S(2)}, u32[]{:S(2)}) async-start(f32[8,52,256]{2,1,0:T(8,128)} %shard_map.93), calls=%async_computation.1 | async-start | bytes 917504 | tf_op jit(solution)/shard_map/all_to_all | solution.py:269
  37.2 0.0 copy-done
  37.2 0.0 copy-start.1
  37.2 1.2 %shard_map.94.column = f32[3,16,256]{2,1,0:T(8,128)S(1)} custom-call(f32[4,13,256]{2,1,0:T(8,128)S(1)} %all_to_all.20.far, f32[4,13,256]{2,1,0:T(8,128)S(1)} %copy-done), custom_call_target="tpu_custom_call" | custom-call | flops 3221225472 | tf_op jit(solution)/shard_map/pallas_call | solution.py:235
  38.3 7.6 %all-to-all-done.1.packed = f32[8,52,256]{2,1,0:T(8,128)S(1)} async-done(((f32[8,52,256]{2,1,0:T(8,128)}), f32[8,52,256]{2,1,0:T(8,128)S(1)}, u32[]{:S(2)}, u32[]{:S(2)}) %all-to-all-start.1) | async-done | bytes 426016 | tf_op jit(solution)/shard_map/all_to_all | solution.py:269
  46.0 0.0 copy-done.1
  46.0 6.8 %shard_map.95 = (f32[32,3,2,128]{3,2,1,0:T(2,128)}, f32[4,3,256]{2,1,0:T(4,128)S(1)}) custom-call(s32[1]{0:T(128)} %bitcast.4.here, f32[8,52,256]{2,1,0:T(8,128)S(1)} %all-to-all-done.1.packed, f32[4,13,256]{2,1,0:T(8,128)S(1)} %copy-done, f32[3,3,256]{2,1,0:T(4,128)S(1)} %copy-done.1, f32[3,16,256]{2,1,0:T(8,128)S(1)} %shard_map.94.column), custom_call_target="tpu_custom_call" | custom-call | tf_op jit(solution)/shard_map/pallas_call | solution.py:235
  52.8 4.4 %all-to-all-start.2 = ((f32[32,3,2,128]{3,2,1,0:T(2,128)}), f32[32,3,2,128]{3,2,1,0:T(2,128)S(1)}, u32[]{:S(2)}, u32[]{:S(2)}) async-start(f32[32,3,2,128]{3,2,1,0:T(2,128)} %get-tuple-element.26), calls=%async_computation.2 | async-start | bytes 196608 | tf_op jit(solution)/shard_map/all_to_all | solution.py:276
  57.2 3.2 %shard_map.96 = (f32[1,3,2,256]{3,2,1,0:T(2,128)}, f32[1,3,2,256]{3,2,1,0:T(2,128)}, f32[6,256]{1,0:T(8,128)S(1)}) custom-call(s32[1]{0:T(128)} %bitcast.here, f32[8,52,256]{2,1,0:T(8,128)S(1)} %all-to-all-done.1.packed, f32[4,13,256]{2,1,0:T(8,128)S(1)} %copy-done, f32[3,3,256]{2,1,0:T(4,128)S(1)} %copy-done.1, f32[4,3,256]{2,1,0:T(4,128)S(1)} %get-tuple-element.20.state), custom_call_target="tpu_custom_call" | custom-call | flops 3221225472 | tf_op jit(solution)/shard_map/pallas_call | solution.py:235
  60.4 3.1 %collective-permute-start = (f32[6,256]{1,0:T(8,128)S(1)}, f32[6,256]{1,0:T(8,128)S(1)}, u32[]{:S(2)}, u32[]{:S(2)}) collective-permute-start(f32[6,256]{1,0:T(8,128)S(1)} %get-tuple-element.23.drift), channel_id=1, source_target_pairs={{0,128},{32,160},{64,192},{96,224},{128,0},{160,32},{192,64},{224,... | collective-permute-start | bytes 18440 | tf_op jit(solution)/shard_map/ppermute | solution.py:285
  63.5 1.6 %collective-permute-done.other = f32[6,256]{1,0:T(8,128)S(1)} collective-permute-done((f32[6,256]{1,0:T(8,128)S(1)}, f32[6,256]{1,0:T(8,128)S(1)}, u32[]{:S(2)}, u32[]{:S(2)}) %collective-permute-start) | collective-permute-done | bytes 6176 | tf_op jit(solution)/shard_map/ppermute | solution.py:285
  65.0 4.6 %collective-permute-start.1 = (f32[6,256]{1,0:T(8,128)S(1)}, f32[6,256]{1,0:T(8,128)S(1)}, u32[]{:S(2)}, u32[]{:S(2)}) collective-permute-start(f32[6,256]{1,0:T(8,128)S(1)} %get-tuple-element.25), channel_id=1, source_target_pairs={{0,256},{32,288},{64,320},{96,352},{128,384},{160,416},{192,448},{... | collective-permute-start | bytes 18440 | tf_op jit(solution)/shard_map/ppermute | solution.py:287
  69.7 1.5 %collective-permute-done.1.other = f32[6,256]{1,0:T(8,128)S(1)} collective-permute-done((f32[6,256]{1,0:T(8,128)S(1)}, f32[6,256]{1,0:T(8,128)S(1)}, u32[]{:S(2)}, u32[]{:S(2)}) %collective-permute-start.1) | collective-permute-done | bytes 6176 | tf_op jit(solution)/shard_map/ppermute | solution.py:287
  71.2 0.6 shard_map.98
  71.9 2.0 %all-to-all-done.2.places = f32[32,3,2,128]{3,2,1,0:T(2,128)S(1)} async-done(((f32[32,3,2,128]{3,2,1,0:T(2,128)}), f32[32,3,2,128]{3,2,1,0:T(2,128)S(1)}, u32[]{:S(2)}, u32[]{:S(2)}) %all-to-all-start.2) | async-done | bytes 98336 | tf_op jit(solution)/shard_map/all_to_all | solution.py:276
  73.9 3.8 %all-to-all-start.3 = ((f32[4,12,256]{2,1,0:T(8,128)}), f32[4,12,256]{2,1,0:T(8,128)S(1)}, u32[]{:S(2)}, u32[]{:S(2)}) async-start(f32[4,12,256]{2,1,0:T(8,128)} %shard_map.98), calls=%async_computation.3 | async-start | bytes 131072 | tf_op jit(solution)/shard_map/all_to_all | solution.py:290
  77.6 0.0 copy-start.2
  77.6 0.0 copy-start.3
  77.6 3.1 %shard_map.99 = f32[3,1,256]{2,1,0:T(1,128)} custom-call(f32[8,52,256]{2,1,0:T(8,128)S(1)} %all-to-all-done.1.packed, f32[32,3,2,128]{3,2,1,0:T(2,128)S(1)} %all-to-all-done.2.places, f32[4,3,256]{2,1,0:T(4,128)S(1)} %get-tuple-element.20.state), custom_call_target="tpu_custom_call" | custom-call | flops 3221225472 | tf_op jit(solution)/shard_map/pallas_call | solution.py:235
  80.8 1.4 %all-to-all-done.3.drift = f32[4,12,256]{2,1,0:T(8,128)S(1)} async-done(((f32[4,12,256]{2,1,0:T(8,128)}), f32[4,12,256]{2,1,0:T(8,128)S(1)}, u32[]{:S(2)}, u32[]{:S(2)}) %all-to-all-start.3) | async-done | bytes 49184 | tf_op jit(solution)/shard_map/all_to_all | solution.py:290
  82.2 0.0 copy-done.2
  82.2 0.0 copy-done.3
  82.2 0.6 shard_map.100
  (1 shorter events, 0.0 us)
Async XLA Ops:
  31.0 6.2 %copy-start = (f32[4,13,256]{2,1,0:T(8,128)S(1)}, f32[4,13,256]{2,1,0:T(8,128)}, u32[]{:S(2)}) copy-start(f32[4,13,256]{2,1,0:T(8,128)} %get-tuple-element.18.own) | copy-start | bytes 159748
  31.0 15.0 %all-to-all-start.1 = ((f32[8,52,256]{2,1,0:T(8,128)}), f32[8,52,256]{2,1,0:T(8,128)S(1)}, u32[]{:S(2)}, u32[]{:S(2)}) async-start(f32[8,52,256]{2,1,0:T(8,128)} %shard_map.93), calls=%async_computation.1 | async-start | bytes 917504 | tf_op jit(solution)/shard_map/all_to_all | solution.py:269
  37.2 8.8 %copy-start.1 = (f32[3,3,256]{2,1,0:T(4,128)S(1)}, f32[3,3,256]{2,1,0:T(4,128)}, u32[]{:S(2)}) copy-start(f32[3,3,256]{2,1,0:T(4,128)} %get-tuple-element.19.known) | copy-start | bytes 27652
  52.8 21.1 %all-to-all-start.2 = ((f32[32,3,2,128]{3,2,1,0:T(2,128)}), f32[32,3,2,128]{3,2,1,0:T(2,128)S(1)}, u32[]{:S(2)}, u32[]{:S(2)}) async-start(f32[32,3,2,128]{3,2,1,0:T(2,128)} %get-tuple-element.26), calls=%async_computation.2 | async-start | bytes 196608 | tf_op jit(solution)/shard_map/all_to_all | solution.py:276
  60.4 4.7 %collective-permute-start = (f32[6,256]{1,0:T(8,128)S(1)}, f32[6,256]{1,0:T(8,128)S(1)}, u32[]{:S(2)}, u32[]{:S(2)}) collective-permute-start(f32[6,256]{1,0:T(8,128)S(1)} %get-tuple-element.23.drift), channel_id=1, source_target_pairs={{0,128},{32,160},{64,192},{96,224},{128,0},{160,32},{192,64},{224,... | collective-permute-start | bytes 18440 | tf_op jit(solution)/shard_map/ppermute | solution.py:285
  65.0 6.2 %collective-permute-start.1 = (f32[6,256]{1,0:T(8,128)S(1)}, f32[6,256]{1,0:T(8,128)S(1)}, u32[]{:S(2)}, u32[]{:S(2)}) collective-permute-start(f32[6,256]{1,0:T(8,128)S(1)} %get-tuple-element.25), channel_id=1, source_target_pairs={{0,256},{32,288},{64,320},{96,352},{128,384},{160,416},{192,448},{... | collective-permute-start | bytes 18440 | tf_op jit(solution)/shard_map/ppermute | solution.py:287
  73.9 8.4 %all-to-all-start.3 = ((f32[4,12,256]{2,1,0:T(8,128)}), f32[4,12,256]{2,1,0:T(8,128)S(1)}, u32[]{:S(2)}, u32[]{:S(2)}) async-start(f32[4,12,256]{2,1,0:T(8,128)} %shard_map.98), calls=%async_computation.3 | async-start | bytes 131072 | tf_op jit(solution)/shard_map/all_to_all | solution.py:290
  77.6 4.6 %copy-start.2 = (f32[3,256]{1,0:T(4,128)S(1)}, f32[3,256]{1,0:T(4,128)}, u32[]{:S(2)}) copy-start(f32[3,256]{1,0:T(4,128)} %places.1) | copy-start | bytes 9220
  77.6 4.6 %copy-start.3 = (f32[3,256]{1,0:T(4,128)S(1)}, f32[3,256]{1,0:T(4,128)}, u32[]{:S(2)}) copy-start(f32[3,256]{1,0:T(4,128)} %speeds.1) | copy-start | bytes 9220

commit v4 on v3

--- a/solution.py
+++ b/solution.py
@@ -135,8 +135,12 @@
             out[k, rows_sent * z : rows_sent * (z + 1)] = far[z]
 
 
-def nodes_of(mine):
-    return [mine[3 * n : 3 * n + 3] for n in range(3)]
+def nodes_of(mine, count):
+    return [mine[3 * n : 3 * n + 3] for n in range(count)]
+
+
+def near_block(here, block):
+    return (here[0] + block + 1) % (ring_y * cores)
 
 
 def column_kernel(far, own, total):
@@ -144,17 +148,17 @@
         return far[z, 3 * node : 3 * node + 3], far[z, 12:13]
 
     total[...] = jnp.zeros_like(total)
-    add_pulls(nodes_of(own[0]), read, 1, total)
+    add_pulls(nodes_of(own[0], 4), read, 1, total)
 
 
 def old_kernel(here, packed, own, known, column, out, state, total):
     def read(node, block, far):
-        near = (here[0] + block + 1) % (ring_y * cores)
+        near = near_block(here, block)
         at = rows_sent * far
         return packed[near, at + 3 * node : at + 3 * node + 3], packed[near, at + 12 : at + 13]
 
-    total[...] = column[...]
-    owns = nodes_of(own[0])
+    total[...] = column[0:3]
+    owns = nodes_of(own[0], 3)
     add_pulls(owns, read, ring_y * cores - 1, total)
     old = forces(owns, total)
     kicks = [slice_length * (w[0] * old[0] + w[1] * old[1] + w[2] * old[2]) for w in lobatto_weights]
@@ -171,33 +175,36 @@
     state[3] = second - known[2]
 
 
-def middle_kernel(here, packed, own, known, state, places, speeds, drift, total):
-    def read(node, near, far):
+def middle_kernel(here, now, packed, own, known, state, column, places, speeds, drift, total):
+    def read(node, block, far):
+        near = near_block(here, block)
         at = rows_sent * far
         return packed[near, at + 9 : at + 12], packed[near, at + 12 : at + 13]
 
     mine = own[0]
-    (force,) = pulls([mine[9:12]], read, total)
+    total[...] = column[3:4]
+    owns = [mine[9:12]]
+    add_pulls(owns, read, ring_y * cores - 1, total)
+    (force,) = forces(owns, total)
     last = state[1] + half_step * force
     for c in range(3):
         places[0, c] = jnp.concatenate([mine[9 + c : 10 + c], state[2, c : c + 1]], axis=0)
         speeds[0, c] = jnp.concatenate([state[0, c : c + 1], last[c : c + 1]], axis=0)
     kick = last - known[0]
-    drift[0:3] = state[3] - (slice_length * here[0].astype(f32)) * kick
+    drift[0:3] = state[3] - (slice_length * now[0].astype(f32)) * kick
     drift[3:6] = kick
 
 
-def pair_kernel(here, drift, other, pair, earlier):
-    got = other[...]
-    pair[...] = drift[...] + got
-    earlier[...] = got * jnp.where((here[0] // line) % 2 == 1, 1.0, 0.0)
-
-
-def four_kernel(here, drift, earlier, other, out):
-    passed = earlier[...] + other[...] * jnp.where(here[0] // line >= 2, 1.0, 0.0)
+def line_kernel(now, drift, *others_and_out):
+    *others, out = others_and_out
+    x = now[0] // line
+    mine = drift[...]
+    passed = jnp.zeros_like(mine)
+    for k, other in enumerate(others):
+        passed = passed + other[...] * jnp.where((x ^ (k + 1)) < x, 1.0, 0.0)
     for k in range(line):
         out[k, 0:6] = passed
-        out[k, 6:12] = drift[...]
+        out[k, 6:12] = mine
 
 
 def end_kernel(packed, places, state, out, total):
@@ -267,30 +274,30 @@
     far = lax.all_to_all(own, "space", 0, 0, axis_index_groups=far_groups(), tiled=True)
     near = run(spread_kernel, shape(ring_y * cores, ring_z * rows_sent, 256))(far)
     packed = lax.all_to_all(near, "space", 0, 0, axis_index_groups=near_groups(), tiled=True)
-    column = run(column_kernel, shape(3, 16, 256), flops=pull_flops)(far, own)
+    column = run(column_kernel, shape(4, 16, 256), flops=pull_flops)(far, own)
     place = lax.axis_index("space").astype(jnp.int32)
     place = ((place // (ring_z * cores)) * cores + place % cores)[None]
     second, state = run(
         old_kernel, (shape(sources, 3, 2, 128), shape(4, 3, 256)), places=(pltpu.SMEM,), scratch=sums(3)
     )(place, packed, own, known, column)
     gathered = lax.all_to_all(second, "space", 0, 0, tiled=True)
-    here = lax.axis_index("tm").astype(jnp.int32)[None]
+    now = lax.axis_index("tm").astype(jnp.int32)[None]
     node_places, node_speeds, drift = run(
         middle_kernel,
         (shape(1, 3, 2, 256), shape(1, 3, 2, 256), shape(6, 256)),
-        places=(pltpu.SMEM,),
+        places=(pltpu.SMEM, pltpu.SMEM),
         scratch=sums(1),
         flops=pull_flops,
-    )(here, packed, own, known, state)
-    other = lax.ppermute(drift, "tm", [(t, t ^ line) for t in range(slices)])
-    pair, earlier = run(pair_kernel, (shape(6, 256), shape(6, 256)), places=(pltpu.SMEM,))(here, drift, other)
-    other = lax.ppermute(pair, "tm", [(t, t ^ (2 * line)) for t in range(slices)])
-    drift = run(four_kernel, shape(line, 12, 256), places=(pltpu.SMEM,))(here, drift, earlier, other)
+    )(place, now, packed, own, known, state, column)
+    others = [
+        lax.ppermute(drift, "tm", [(t, t ^ (k * line)) for t in range(slices)]) for k in range(1, slices // line)
+    ]
+    drift = run(line_kernel, shape(line, 12, 256), places=(pltpu.SMEM,))(now, drift, *others)
     drift, gathered = lax.optimization_barrier((drift, gathered))
     drift = lax.all_to_all(drift, "tm", 0, 0, axis_index_groups=line_groups(), tiled=True)
     end_force = run(end_kernel, shape(3, 1, 256), scratch=sums(1), flops=pull_flops)(packed, gathered, state)
     start_places, start_speeds = run(start_kernel, (shape(3, 1, 256), shape(3, 1, 256)), places=(pltpu.SMEM,))(
-        here, drift, initial_places, initial_speeds
+        now, drift, initial_places, initial_speeds
     )
     return (
         node_places.transpose(0, 2, 1, 3),

time: 83.9 us -> 84 us (level)
  waiting for transfers between devices: 14.2 us -> 12.9 us
  starting transfers between devices: 22.1 us -> 23.3 us
    ppermute x2 -> x3, starting transfers between devices: 7.75 us -> 8.97 us  [body(): lax.ppermute(drift, 'tm', [(t, t ^ k * line) for t in range(slices)])]
    ppermute x2 -> x3, waiting for transfers between devices: 3.09 us -> 2.51 us  [body(): lax.ppermute(drift, 'tm', [(t, t ^ k * line) for t in range(slices)])]
    pallas_call x9 -> x8, Pallas kernels: 17.8 us -> 17.8 us  [call(): pl.pallas_call(kernel, in_specs=specs, out_shape=outs, scratch_shapes=lis...]
  transfers between devices with their start and end apart: 5 -> 6, of which waited for: 5 -> 5; matrix products, arithmetic and copies ran while one was open for 0% -> 0% of each run, Pallas kernels for 10% -> 10%
where the time goes in v4:
time: 84 us; the launch traced here: 82.8 us
  blocking collectives  28.1 us (33%)
  starting transfers between devices  23.3 us (28%)
  Pallas kernels  17.8 us (21%)
  waiting for transfers between devices  12.9 us (15%)
    all_to_all x1, blocking collectives, body(): lax.all_to_all(own, 'space', 0, 0, axis_index_groups=far_groups(), tiled=...  28.1 us
    pallas_call x8, Pallas kernels, call(): pl.pallas_call(kernel, in_specs=specs, out_shape=outs, scratch_shapes=lis...  17.8 us
    ppermute x3, starting transfers between devices, body(): lax.ppermute(drift, 'tm', [(t, t ^ k * line) for t in range(slices)])  8.97 us
    all_to_all x1, waiting for transfers between devices, body(): lax.all_to_all(near, 'space', 0, 0, axis_index_groups=near_groups(), tile...  7.34 us
    all_to_all x1, starting transfers between devices, body(): lax.all_to_all(near, 'space', 0, 0, axis_index_groups=near_groups(), tile...  6.19 us
    all_to_all x1, starting transfers between devices, body(): gathered = lax.all_to_all(second, 'space', 0, 0, tiled=True)  4.37 us
    all_to_all x1, starting transfers between devices, body(): lax.all_to_all(drift, 'tm', 0, 0, axis_index_groups=line_groups(), tiled=...  3.76 us
    ppermute x3, waiting for transfers between devices, body(): lax.ppermute(drift, 'tm', [(t, t ^ k * line) for t in range(slices)])  2.51 us
  transfers between devices with their start and end apart: 6, of which 5 were waited for; matrix products, arithmetic and copies ran while one was open for 0% of the time, Pallas kernels for 10%

profile of v4, /device:TPU:1, one launch (start us, length us, event | category | flops | bytes accessed | tf_op | source)
XLA Modules:
  0.0 82.8 jit_solution(4910908796872222761)
XLA Ops:
  0.6 1.4 %shard_map.92 = (f32[4,13,256]{2,1,0:T(8,128)}, f32[3,3,256]{2,1,0:T(4,128)}) custom-call(f32[3,3,1,256]{3,2,1,0:T(1,128)} %bitcast.10, f32[3,3,1,256]{3,2,1,0:T(1,128)} %bitcast.11, f32[1,256]{1,0:T(1,128)} %bitcast.12), custom_call_target="tpu_custom_call" | custom-call | tf_op jit(solution)/shard_map/pallas_call | solution.py:242
  2.0 28.1 %all_to_all.20.far = f32[4,13,256]{2,1,0:T(8,128)S(1)} all-to-all(f32[4,13,256]{2,1,0:T(8,128)} %get-tuple-element.16.own), channel_id=1, replica_groups={{0,2,4,6},{1,3,5,7},{8,10,12,14},{9,11,13,15},{16,18,20,22},{17,19,21,2..., dimensions={0} | all-to-all | bytes 106496 | tf_op jit(solution)/shard_map/all_to_all | solution.py:274
  30.2 0.8 shard_map.93
  31.0 0.0 copy-start
  31.0 6.2 %all-to-all-start.1 = ((f32[8,52,256]{2,1,0:T(8,128)}), f32[8,52,256]{2,1,0:T(8,128)S(1)}, u32[]{:S(2)}, u32[]{:S(2)}) async-start(f32[8,52,256]{2,1,0:T(8,128)} %shard_map.93), calls=%async_computation.1 | async-start | bytes 917504 | tf_op jit(solution)/shard_map/all_to_all | solution.py:276
  37.2 0.0 copy-done
  37.2 0.0 copy-start.1
  37.2 1.4 %shard_map.94.column = f32[4,16,256]{2,1,0:T(8,128)S(1)} custom-call(f32[4,13,256]{2,1,0:T(8,128)S(1)} %all_to_all.20.far, f32[4,13,256]{2,1,0:T(8,128)S(1)} %copy-done), custom_call_target="tpu_custom_call" | custom-call | flops 3221225472 | tf_op jit(solution)/shard_map/pallas_call | solution.py:242
  38.6 7.3 %all-to-all-done.1.packed = f32[8,52,256]{2,1,0:T(8,128)S(1)} async-done(((f32[8,52,256]{2,1,0:T(8,128)}), f32[8,52,256]{2,1,0:T(8,128)S(1)}, u32[]{:S(2)}, u32[]{:S(2)}) %all-to-all-start.1) | async-done | bytes 426016 | tf_op jit(solution)/shard_map/all_to_all | solution.py:276
  46.0 0.0 copy-done.1
  46.0 6.8 %shard_map.95 = (f32[32,3,2,128]{3,2,1,0:T(2,128)}, f32[4,3,256]{2,1,0:T(4,128)S(1)}) custom-call(s32[1]{0:T(128)} %bitcast.here, f32[8,52,256]{2,1,0:T(8,128)S(1)} %all-to-all-done.1.packed, f32[4,13,256]{2,1,0:T(8,128)S(1)} %copy-done, f32[3,3,256]{2,1,0:T(4,128)S(1)} %copy-done.1, f32[4,16,256]{2,1,0:T(8,128)S(1)} %shard_map.94.column), custom_call_target="tpu_custom_call" | custom-call | tf_op jit(solution)/shard_map/pallas_call | solution.py:242
  52.8 4.4 %all-to-all-start.2 = ((f32[32,3,2,128]{3,2,1,0:T(2,128)}), f32[32,3,2,128]{3,2,1,0:T(2,128)S(1)}, u32[]{:S(2)}, u32[]{:S(2)}) async-start(f32[32,3,2,128]{3,2,1,0:T(2,128)} %get-tuple-element.22), calls=%async_computation.2 | async-start | bytes 196608 | tf_op jit(solution)/shard_map/all_to_all | solution.py:283
  57.2 2.9 %shard_map.96 = (f32[1,3,2,256]{3,2,1,0:T(2,128)}, f32[1,3,2,256]{3,2,1,0:T(2,128)}, f32[6,256]{1,0:T(8,128)S(1)}) custom-call(s32[1]{0:T(128)} %bitcast.here, s32[1]{0:T(128)} %bitcast.1.now.here, f32[8,52,256]{2,1,0:T(8,128)S(1)} %all-to-all-done.1.packed, f32[4,13,256]{2,1,0:T(8,128)S(1)} %copy-done, f32[3,3,256]{2,1,0:T(4,128)S(1)} %copy-done.1, ...), custom_call_target="tpu_custom_call" | custom-call | flops 3221225472 | tf_op jit(solution)/shard_map/pallas_call | solution.py:242
  60.1 4.4 %collective-permute-start.2 = (f32[6,256]{1,0:T(8,128)S(1)}, f32[6,256]{1,0:T(8,128)S(1)}, u32[]{:S(2)}, u32[]{:S(2)}) collective-permute-start(f32[6,256]{1,0:T(8,128)S(1)} %get-tuple-element.21.drift), channel_id=1, source_target_pairs={{0,384},{32,416},{64,448},{96,480},{128,256},{160,288},{192,320},{... | collective-permute-start | bytes 18440 | tf_op jit(solution)/shard_map/ppermute | solution.py:293
  64.5 2.4 %collective-permute-start.1 = (f32[6,256]{1,0:T(8,128)S(1)}, f32[6,256]{1,0:T(8,128)S(1)}, u32[]{:S(2)}, u32[]{:S(2)}) collective-permute-start(f32[6,256]{1,0:T(8,128)S(1)} %get-tuple-element.21.drift), channel_id=1, source_target_pairs={{0,256},{32,288},{64,320},{96,352},{128,384},{160,416},{192,448},{... | collective-permute-start | bytes 18440 | tf_op jit(solution)/shard_map/ppermute | solution.py:293
  66.9 2.2 %collective-permute-start = (f32[6,256]{1,0:T(8,128)S(1)}, f32[6,256]{1,0:T(8,128)S(1)}, u32[]{:S(2)}, u32[]{:S(2)}) collective-permute-start(f32[6,256]{1,0:T(8,128)S(1)} %get-tuple-element.21.drift), channel_id=1, source_target_pairs={{0,128},{32,160},{64,192},{96,224},{128,0},{160,32},{192,64},{224,... | collective-permute-start | bytes 18440 | tf_op jit(solution)/shard_map/ppermute | solution.py:293
  69.1 0.0 collective-permute-done.2.others_and_out_2_
  69.1 1.6 %collective-permute-done.1.others_and_out_1_ = f32[6,256]{1,0:T(8,128)S(1)} collective-permute-done((f32[6,256]{1,0:T(8,128)S(1)}, f32[6,256]{1,0:T(8,128)S(1)}, u32[]{:S(2)}, u32[]{:S(2)}) %collective-permute-start.1) | collective-permute-done | bytes 6176 | tf_op jit(solution)/shard_map/ppermute | solution.py:293
  70.7 0.9 %collective-permute-done.others_and_out_0_ = f32[6,256]{1,0:T(8,128)S(1)} collective-permute-done((f32[6,256]{1,0:T(8,128)S(1)}, f32[6,256]{1,0:T(8,128)S(1)}, u32[]{:S(2)}, u32[]{:S(2)}) %collective-permute-start) | collective-permute-done | bytes 6176 | tf_op jit(solution)/shard_map/ppermute | solution.py:293
  71.6 0.6 shard_map.97
  72.2 1.6 %all-to-all-done.2.places = f32[32,3,2,128]{3,2,1,0:T(2,128)S(1)} async-done(((f32[32,3,2,128]{3,2,1,0:T(2,128)}), f32[32,3,2,128]{3,2,1,0:T(2,128)S(1)}, u32[]{:S(2)}, u32[]{:S(2)}) %all-to-all-start.2) | async-done | bytes 98336 | tf_op jit(solution)/shard_map/all_to_all | solution.py:283
  73.9 3.8 %all-to-all-start.3 = ((f32[4,12,256]{2,1,0:T(8,128)}), f32[4,12,256]{2,1,0:T(8,128)S(1)}, u32[]{:S(2)}, u32[]{:S(2)}) async-start(f32[4,12,256]{2,1,0:T(8,128)} %shard_map.97), calls=%async_computation.3 | async-start | bytes 131072 | tf_op jit(solution)/shard_map/all_to_all | solution.py:297
  77.6 0.0 copy-start.2
  77.6 0.0 copy-start.3
  77.6 3.1 %shard_map.98 = f32[3,1,256]{2,1,0:T(1,128)} custom-call(f32[8,52,256]{2,1,0:T(8,128)S(1)} %all-to-all-done.1.packed, f32[32,3,2,128]{3,2,1,0:T(2,128)S(1)} %all-to-all-done.2.places, f32[4,3,256]{2,1,0:T(4,128)S(1)} %get-tuple-element.18.state), custom_call_target="tpu_custom_call" | custom-call | flops 3221225472 | tf_op jit(solution)/shard_map/pallas_call | solution.py:242
  80.8 1.4 %all-to-all-done.3.drift = f32[4,12,256]{2,1,0:T(8,128)S(1)} async-done(((f32[4,12,256]{2,1,0:T(8,128)}), f32[4,12,256]{2,1,0:T(8,128)S(1)}, u32[]{:S(2)}, u32[]{:S(2)}) %all-to-all-start.3) | async-done | bytes 49184 | tf_op jit(solution)/shard_map/all_to_all | solution.py:297
  82.2 0.0 copy-done.2
  82.2 0.0 copy-done.3
  82.2 0.6 shard_map.99
Async XLA Ops:
  31.0 6.2 %copy-start = (f32[4,13,256]{2,1,0:T(8,128)S(1)}, f32[4,13,256]{2,1,0:T(8,128)}, u32[]{:S(2)}) copy-start(f32[4,13,256]{2,1,0:T(8,128)} %get-tuple-element.16.own) | copy-start | bytes 159748
  31.0 15.0 %all-to-all-start.1 = ((f32[8,52,256]{2,1,0:T(8,128)}), f32[8,52,256]{2,1,0:T(8,128)S(1)}, u32[]{:S(2)}, u32[]{:S(2)}) async-start(f32[8,52,256]{2,1,0:T(8,128)} %shard_map.93), calls=%async_computation.1 | async-start | bytes 917504 | tf_op jit(solution)/shard_map/all_to_all | solution.py:276
  37.2 8.8 %copy-start.1 = (f32[3,3,256]{2,1,0:T(4,128)S(1)}, f32[3,3,256]{2,1,0:T(4,128)}, u32[]{:S(2)}) copy-start(f32[3,3,256]{2,1,0:T(4,128)} %get-tuple-element.17.known) | copy-start | bytes 27652
  52.8 21.1 %all-to-all-start.2 = ((f32[32,3,2,128]{3,2,1,0:T(2,128)}), f32[32,3,2,128]{3,2,1,0:T(2,128)S(1)}, u32[]{:S(2)}, u32[]{:S(2)}) async-start(f32[32,3,2,128]{3,2,1,0:T(2,128)} %get-tuple-element.22), calls=%async_computation.2 | async-start | bytes 196608 | tf_op jit(solution)/shard_map/all_to_all | solution.py:283
  60.1 9.0 %collective-permute-start.2 = (f32[6,256]{1,0:T(8,128)S(1)}, f32[6,256]{1,0:T(8,128)S(1)}, u32[]{:S(2)}, u32[]{:S(2)}) collective-permute-start(f32[6,256]{1,0:T(8,128)S(1)} %get-tuple-element.21.drift), channel_id=1, source_target_pairs={{0,384},{32,416},{64,448},{96,480},{128,256},{160,288},{192,320},{... | collective-permute-start | bytes 18440 | tf_op jit(solution)/shard_map/ppermute | solution.py:293
  64.5 6.2 %collective-permute-start.1 = (f32[6,256]{1,0:T(8,128)S(1)}, f32[6,256]{1,0:T(8,128)S(1)}, u32[]{:S(2)}, u32[]{:S(2)}) collective-permute-start(f32[6,256]{1,0:T(8,128)S(1)} %get-tuple-element.21.drift), channel_id=1, source_target_pairs={{0,256},{32,288},{64,320},{96,352},{128,384},{160,416},{192,448},{... | collective-permute-start | bytes 18440 | tf_op jit(solution)/shard_map/ppermute | solution.py:293
  66.9 4.7 %collective-permute-start = (f32[6,256]{1,0:T(8,128)S(1)}, f32[6,256]{1,0:T(8,128)S(1)}, u32[]{:S(2)}, u32[]{:S(2)}) collective-permute-start(f32[6,256]{1,0:T(8,128)S(1)} %get-tuple-element.21.drift), channel_id=1, source_target_pairs={{0,128},{32,160},{64,192},{96,224},{128,0},{160,32},{192,64},{224,... | collective-permute-start | bytes 18440 | tf_op jit(solution)/shard_map/ppermute | solution.py:293
  73.9 8.4 %all-to-all-start.3 = ((f32[4,12,256]{2,1,0:T(8,128)}), f32[4,12,256]{2,1,0:T(8,128)S(1)}, u32[]{:S(2)}, u32[]{:S(2)}) async-start(f32[4,12,256]{2,1,0:T(8,128)} %shard_map.97), calls=%async_computation.3 | async-start | bytes 131072 | tf_op jit(solution)/shard_map/all_to_all | solution.py:297
  77.6 4.6 %copy-start.2 = (f32[3,256]{1,0:T(4,128)S(1)}, f32[3,256]{1,0:T(4,128)}, u32[]{:S(2)}) copy-start(f32[3,256]{1,0:T(4,128)} %places.1) | copy-start | bytes 9220
  77.6 4.6 %copy-start.3 = (f32[3,256]{1,0:T(4,128)S(1)}, f32[3,256]{1,0:T(4,128)}, u32[]{:S(2)}) copy-start(f32[3,256]{1,0:T(4,128)} %speeds.1) | copy-start | bytes 9220

commit v5 on v4

--- a/solution.py
+++ b/solution.py
@@ -130,13 +130,19 @@
 
 
 def spread_kernel(far, out):
-    for k in range(ring_y * cores):
-        for z in range(ring_z):
-            out[k, rows_sent * z : rows_sent * (z + 1)] = far[z]
+    for row in range(rows_sent):
+        line_of = jnp.concatenate([far[z, row : row + 1] for z in range(ring_z)], axis=0)
+        for k in range(ring_y * cores):
+            out[k, row] = line_of
 
 
 def nodes_of(mine, count):
     return [mine[3 * n : 3 * n + 3] for n in range(count)]
+
+
+def rows_of(packed, near, far, first):
+    places = [packed[near, first + c, far : far + 1] for c in range(3)]
+    return jnp.concatenate(places, axis=0), packed[near, 12, far : far + 1]
 
 
 def near_block(here, block):
@@ -154,8 +160,7 @@
 def old_kernel(here, packed, own, known, column, out, state, total):
     def read(node, block, far):
         near = near_block(here, block)
-        at = rows_sent * far
-        return packed[near, at + 3 * node : at + 3 * node + 3], packed[near, at + 12 : at + 13]
+        return rows_of(packed, near, far, 3 * node)
 
     total[...] = column[0:3]
     owns = nodes_of(own[0], 3)
@@ -178,8 +183,7 @@
 def middle_kernel(here, now, packed, own, known, state, column, places, speeds, drift, total):
     def read(node, block, far):
         near = near_block(here, block)
-        at = rows_sent * far
-        return packed[near, at + 9 : at + 12], packed[near, at + 12 : at + 13]
+        return rows_of(packed, near, far, 9)
 
     mine = own[0]
     total[...] = column[3:4]
@@ -211,8 +215,7 @@
     def read(node, near, far):
         source = (near // cores) * (ring_z * cores) + far * cores + near % cores
         halves = [jnp.concatenate([places[source, c, h : h + 1] for c in range(3)], axis=0) for h in range(2)]
-        at = rows_sent * far
-        return jnp.concatenate(halves, axis=1), packed[near, at + 12 : at + 13]
+        return jnp.concatenate(halves, axis=1), packed[near, 12, far : far + 1]
 
     (force,) = pulls([state[2]], read, total)
     for c in range(3):
@@ -272,7 +275,7 @@
         room=60,
     )(positions, velocities, masses)
     far = lax.all_to_all(own, "space", 0, 0, axis_index_groups=far_groups(), tiled=True)
-    near = run(spread_kernel, shape(ring_y * cores, ring_z * rows_sent, 256))(far)
+    near = run(spread_kernel, shape(ring_y * cores, rows_sent, ring_z, 256))(far)
     packed = lax.all_to_all(near, "space", 0, 0, axis_index_groups=near_groups(), tiled=True)
     column = run(column_kernel, shape(4, 16, 256), flops=pull_flops)(far, own)
     place = lax.axis_index("space").astype(jnp.int32)

time: 84 us -> 83.6 us (level)
  no operation moved by 1% of the time
where the time goes in v5:
time: 83.6 us; the launch traced here: 82.4 us
  blocking collectives  28.1 us (34%)
  starting transfers between devices  23.3 us (28%)
  Pallas kernels  17.7 us (21%)
  waiting for transfers between devices  12.6 us (15%)
    all_to_all x1, blocking collectives, body(): lax.all_to_all(own, 'space', 0, 0, axis_index_groups=far_groups(), tiled=...  28.1 us
    pallas_call x8, Pallas kernels, call(): pl.pallas_call(kernel, in_specs=specs, out_shape=outs, scratch_shapes=lis...  17.7 us
    ppermute x3, starting transfers between devices, body(): lax.ppermute(drift, 'tm', [(t, t ^ k * line) for t in range(slices)])  8.97 us
    all_to_all x1, waiting for transfers between devices, body(): lax.all_to_all(near, 'space', 0, 0, axis_index_groups=near_groups(), tile...  6.99 us
    all_to_all x1, starting transfers between devices, body(): lax.all_to_all(near, 'space', 0, 0, axis_index_groups=near_groups(), tile...  6.19 us
    all_to_all x1, starting transfers between devices, body(): gathered = lax.all_to_all(second, 'space', 0, 0, tiled=True)  4.37 us
    all_to_all x1, starting transfers between devices, body(): lax.all_to_all(drift, 'tm', 0, 0, axis_index_groups=line_groups(), tiled=...  3.76 us
    ppermute x3, waiting for transfers between devices, body(): lax.ppermute(drift, 'tm', [(t, t ^ k * line) for t in range(slices)])  2.51 us
  transfers between devices with their start and end apart: 6, of which 5 were waited for; matrix products, arithmetic and copies ran while one was open for 0% of the time, Pallas kernels for 10%

profile of v5, /device:TPU:1, one launch (start us, length us, event | category | flops | bytes accessed | tf_op | source)
XLA Modules:
  0.0 82.4 jit_solution(7945447458262799747)
XLA Ops:
  0.6 1.4 %shard_map.92 = (f32[4,13,256]{2,1,0:T(8,128)}, f32[3,3,256]{2,1,0:T(4,128)}) custom-call(f32[3,3,1,256]{3,2,1,0:T(1,128)} %bitcast.10, f32[3,3,1,256]{3,2,1,0:T(1,128)} %bitcast.11, f32[1,256]{1,0:T(1,128)} %bitcast.12), custom_call_target="tpu_custom_call" | custom-call | tf_op jit(solution)/shard_map/pallas_call | solution.py:245
  2.0 28.1 %all_to_all.20.far = f32[4,13,256]{2,1,0:T(8,128)S(1)} all-to-all(f32[4,13,256]{2,1,0:T(8,128)} %get-tuple-element.16.own), channel_id=1, replica_groups={{0,2,4,6},{1,3,5,7},{8,10,12,14},{9,11,13,15},{16,18,20,22},{17,19,21,2..., dimensions={0} | all-to-all | bytes 106496 | tf_op jit(solution)/shard_map/all_to_all | solution.py:277
  30.2 0.8 shard_map.93
  31.0 0.0 copy-start
  31.0 6.2 %all-to-all-start.1 = ((f32[8,13,4,256]{3,2,1,0:T(4,128)}), f32[8,13,4,256]{3,2,1,0:T(4,128)S(1)}, u32[]{:S(2)}, u32[]{:S(2)}) async-start(f32[8,13,4,256]{3,2,1,0:T(4,128)} %shard_map.93), calls=%async_computation.1 | async-start | bytes 851968 | tf_op jit(solution)/shard_map/all_to_all | solution.py:279
  37.2 0.0 copy-done
  37.2 0.0 copy-start.1
  37.2 1.4 %shard_map.94.column = f32[4,16,256]{2,1,0:T(8,128)S(1)} custom-call(f32[4,13,256]{2,1,0:T(8,128)S(1)} %all_to_all.20.far, f32[4,13,256]{2,1,0:T(8,128)S(1)} %copy-done), custom_call_target="tpu_custom_call" | custom-call | flops 3221225472 | tf_op jit(solution)/shard_map/pallas_call | solution.py:245
  38.6 7.0 %all-to-all-done.1.packed = f32[8,13,4,256]{3,2,1,0:T(4,128)S(1)} async-done(((f32[8,13,4,256]{3,2,1,0:T(4,128)}), f32[8,13,4,256]{3,2,1,0:T(4,128)S(1)}, u32[]{:S(2)}, u32[]{:S(2)}) %all-to-all-start.1) | async-done | bytes 426016 | tf_op jit(solution)/shard_map/all_to_all | solution.py:279
  45.6 0.0 copy-done.1
  45.6 6.8 %shard_map.95 = (f32[32,3,2,128]{3,2,1,0:T(2,128)}, f32[4,3,256]{2,1,0:T(4,128)S(1)}) custom-call(s32[1]{0:T(128)} %bitcast.here, f32[8,13,4,256]{3,2,1,0:T(4,128)S(1)} %all-to-all-done.1.packed, f32[4,13,256]{2,1,0:T(8,128)S(1)} %copy-done, f32[3,3,256]{2,1,0:T(4,128)S(1)} %copy-done.1, f32[4,16,256]{2,1,0:T(8,128)S(1)} %shard_map.94.column), custom_call_target="tpu_custom_call" | custom-call | tf_op jit(solution)/shard_map/pallas_call | solution.py:245
  52.4 4.4 %all-to-all-start.2 = ((f32[32,3,2,128]{3,2,1,0:T(2,128)}), f32[32,3,2,128]{3,2,1,0:T(2,128)S(1)}, u32[]{:S(2)}, u32[]{:S(2)}) async-start(f32[32,3,2,128]{3,2,1,0:T(2,128)} %get-tuple-element.22), calls=%async_computation.2 | async-start | bytes 196608 | tf_op jit(solution)/shard_map/all_to_all | solution.py:286
  56.8 2.9 %shard_map.96 = (f32[1,3,2,256]{3,2,1,0:T(2,128)}, f32[1,3,2,256]{3,2,1,0:T(2,128)}, f32[6,256]{1,0:T(8,128)S(1)}) custom-call(s32[1]{0:T(128)} %bitcast.here, s32[1]{0:T(128)} %bitcast.1.now.here, f32[8,13,4,256]{3,2,1,0:T(4,128)S(1)} %all-to-all-done.1.packed, f32[4,13,256]{2,1,0:T(8,128)S(1)} %copy-done, f32[3,3,256]{2,1,0:T(4,128)S(1)} %copy-done.1, ...), custom_call_target="tpu_custom_call" | custom-call | flops 3221225472 | tf_op jit(solution)/shard_map/pallas_call | solution.py:245
  59.7 4.4 %collective-permute-start.2 = (f32[6,256]{1,0:T(8,128)S(1)}, f32[6,256]{1,0:T(8,128)S(1)}, u32[]{:S(2)}, u32[]{:S(2)}) collective-permute-start(f32[6,256]{1,0:T(8,128)S(1)} %get-tuple-element.21.drift), channel_id=1, source_target_pairs={{0,384},{32,416},{64,448},{96,480},{128,256},{160,288},{192,320},{... | collective-permute-start | bytes 18440 | tf_op jit(solution)/shard_map/ppermute | solution.py:296
  64.1 2.4 %collective-permute-start.1 = (f32[6,256]{1,0:T(8,128)S(1)}, f32[6,256]{1,0:T(8,128)S(1)}, u32[]{:S(2)}, u32[]{:S(2)}) collective-permute-start(f32[6,256]{1,0:T(8,128)S(1)} %get-tuple-element.21.drift), channel_id=1, source_target_pairs={{0,256},{32,288},{64,320},{96,352},{128,384},{160,416},{192,448},{... | collective-permute-start | bytes 18440 | tf_op jit(solution)/shard_map/ppermute | solution.py:296
  66.5 2.2 %collective-permute-start = (f32[6,256]{1,0:T(8,128)S(1)}, f32[6,256]{1,0:T(8,128)S(1)}, u32[]{:S(2)}, u32[]{:S(2)}) collective-permute-start(f32[6,256]{1,0:T(8,128)S(1)} %get-tuple-element.21.drift), channel_id=1, source_target_pairs={{0,128},{32,160},{64,192},{96,224},{128,0},{160,32},{192,64},{224,... | collective-permute-start | bytes 18440 | tf_op jit(solution)/shard_map/ppermute | solution.py:296
  68.7 0.0 collective-permute-done.2.others_and_out_2_
  68.7 1.6 %collective-permute-done.1.others_and_out_1_ = f32[6,256]{1,0:T(8,128)S(1)} collective-permute-done((f32[6,256]{1,0:T(8,128)S(1)}, f32[6,256]{1,0:T(8,128)S(1)}, u32[]{:S(2)}, u32[]{:S(2)}) %collective-permute-start.1) | collective-permute-done | bytes 6176 | tf_op jit(solution)/shard_map/ppermute | solution.py:296
  70.3 0.9 %collective-permute-done.others_and_out_0_ = f32[6,256]{1,0:T(8,128)S(1)} collective-permute-done((f32[6,256]{1,0:T(8,128)S(1)}, f32[6,256]{1,0:T(8,128)S(1)}, u32[]{:S(2)}, u32[]{:S(2)}) %collective-permute-start) | collective-permute-done | bytes 6176 | tf_op jit(solution)/shard_map/ppermute | solution.py:296
  71.2 0.6 shard_map.97
  71.8 1.6 %all-to-all-done.2.places = f32[32,3,2,128]{3,2,1,0:T(2,128)S(1)} async-done(((f32[32,3,2,128]{3,2,1,0:T(2,128)}), f32[32,3,2,128]{3,2,1,0:T(2,128)S(1)}, u32[]{:S(2)}, u32[]{:S(2)}) %all-to-all-start.2) | async-done | bytes 98336 | tf_op jit(solution)/shard_map/all_to_all | solution.py:286
  73.5 3.8 %all-to-all-start.3 = ((f32[4,12,256]{2,1,0:T(8,128)}), f32[4,12,256]{2,1,0:T(8,128)S(1)}, u32[]{:S(2)}, u32[]{:S(2)}) async-start(f32[4,12,256]{2,1,0:T(8,128)} %shard_map.97), calls=%async_computation.3 | async-start | bytes 131072 | tf_op jit(solution)/shard_map/all_to_all | solution.py:300
  77.2 0.0 copy-start.2
  77.2 0.0 copy-start.3
  77.2 3.1 %shard_map.98 = f32[3,1,256]{2,1,0:T(1,128)} custom-call(f32[8,13,4,256]{3,2,1,0:T(4,128)S(1)} %all-to-all-done.1.packed, f32[32,3,2,128]{3,2,1,0:T(2,128)S(1)} %all-to-all-done.2.places, f32[4,3,256]{2,1,0:T(4,128)S(1)} %get-tuple-element.18.state), custom_call_target="tpu_custom_call" | custom-call | flops 3221225472 | tf_op jit(solution)/shard_map/pallas_call | solution.py:245
  80.4 1.4 %all-to-all-done.3.drift = f32[4,12,256]{2,1,0:T(8,128)S(1)} async-done(((f32[4,12,256]{2,1,0:T(8,128)}), f32[4,12,256]{2,1,0:T(8,128)S(1)}, u32[]{:S(2)}, u32[]{:S(2)}) %all-to-all-start.3) | async-done | bytes 49184 | tf_op jit(solution)/shard_map/all_to_all | solution.py:300
  81.8 0.0 copy-done.2
  81.8 0.0 copy-done.3
  81.8 0.6 shard_map.99
Async XLA Ops:
  31.0 6.2 %copy-start = (f32[4,13,256]{2,1,0:T(8,128)S(1)}, f32[4,13,256]{2,1,0:T(8,128)}, u32[]{:S(2)}) copy-start(f32[4,13,256]{2,1,0:T(8,128)} %get-tuple-element.16.own) | copy-start | bytes 159748
  31.0 14.6 %all-to-all-start.1 = ((f32[8,13,4,256]{3,2,1,0:T(4,128)}), f32[8,13,4,256]{3,2,1,0:T(4,128)S(1)}, u32[]{:S(2)}, u32[]{:S(2)}) async-start(f32[8,13,4,256]{3,2,1,0:T(4,128)} %shard_map.93), calls=%async_computation.1 | async-start | bytes 851968 | tf_op jit(solution)/shard_map/all_to_all | solution.py:279
  37.2 8.4 %copy-start.1 = (f32[3,3,256]{2,1,0:T(4,128)S(1)}, f32[3,3,256]{2,1,0:T(4,128)}, u32[]{:S(2)}) copy-start(f32[3,3,256]{2,1,0:T(4,128)} %get-tuple-element.17.known) | copy-start | bytes 27652
  52.4 21.1 %all-to-all-start.2 = ((f32[32,3,2,128]{3,2,1,0:T(2,128)}), f32[32,3,2,128]{3,2,1,0:T(2,128)S(1)}, u32[]{:S(2)}, u32[]{:S(2)}) async-start(f32[32,3,2,128]{3,2,1,0:T(2,128)} %get-tuple-element.22), calls=%async_computation.2 | async-start | bytes 196608 | tf_op jit(solution)/shard_map/all_to_all | solution.py:286
  59.7 9.0 %collective-permute-start.2 = (f32[6,256]{1,0:T(8,128)S(1)}, f32[6,256]{1,0:T(8,128)S(1)}, u32[]{:S(2)}, u32[]{:S(2)}) collective-permute-start(f32[6,256]{1,0:T(8,128)S(1)} %get-tuple-element.21.drift), channel_id=1, source_target_pairs={{0,384},{32,416},{64,448},{96,480},{128,256},{160,288},{192,320},{... | collective-permute-start | bytes 18440 | tf_op jit(solution)/shard_map/ppermute | solution.py:296
  64.1 6.2 %collective-permute-start.1 = (f32[6,256]{1,0:T(8,128)S(1)}, f32[6,256]{1,0:T(8,128)S(1)}, u32[]{:S(2)}, u32[]{:S(2)}) collective-permute-start(f32[6,256]{1,0:T(8,128)S(1)} %get-tuple-element.21.drift), channel_id=1, source_target_pairs={{0,256},{32,288},{64,320},{96,352},{128,384},{160,416},{192,448},{... | collective-permute-start | bytes 18440 | tf_op jit(solution)/shard_map/ppermute | solution.py:296
  66.5 4.7 %collective-permute-start = (f32[6,256]{1,0:T(8,128)S(1)}, f32[6,256]{1,0:T(8,128)S(1)}, u32[]{:S(2)}, u32[]{:S(2)}) collective-permute-start(f32[6,256]{1,0:T(8,128)S(1)} %get-tuple-element.21.drift), channel_id=1, source_target_pairs={{0,128},{32,160},{64,192},{96,224},{128,0},{160,32},{192,64},{224,... | collective-permute-start | bytes 18440 | tf_op jit(solution)/shard_map/ppermute | solution.py:296
  73.5 8.4 %all-to-all-start.3 = ((f32[4,12,256]{2,1,0:T(8,128)}), f32[4,12,256]{2,1,0:T(8,128)S(1)}, u32[]{:S(2)}, u32[]{:S(2)}) async-start(f32[4,12,256]{2,1,0:T(8,128)} %shard_map.97), calls=%async_computation.3 | async-start | bytes 131072 | tf_op jit(solution)/shard_map/all_to_all | solution.py:300
  77.2 4.6 %copy-start.2 = (f32[3,256]{1,0:T(4,128)S(1)}, f32[3,256]{1,0:T(4,128)}, u32[]{:S(2)}) copy-start(f32[3,256]{1,0:T(4,128)} %places.1) | copy-start | bytes 9220
  77.2 4.6 %copy-start.3 = (f32[3,256]{1,0:T(4,128)S(1)}, f32[3,256]{1,0:T(4,128)}, u32[]{:S(2)}) copy-start(f32[3,256]{1,0:T(4,128)} %speeds.1) | copy-start | bytes 9220

commit v6 on v5

--- a/solution.py
+++ b/solution.py
@@ -15,6 +15,7 @@
 sources = 32
 slices = 16
 ring_y, ring_z, cores = 4, 4, 2
+column = ring_z * cores
 line = 4
 rows_sent = 13
 f32 = jnp.float32
@@ -23,13 +24,11 @@
 
 
 def far_groups():
-    places = np.arange(sources).reshape(ring_y, ring_z, cores)
-    return [[int(p) for p in places[y, :, c]] for y in range(ring_y) for c in range(cores)]
+    return [[y * column + k for k in range(column)] for y in range(ring_y)]
 
 
 def near_groups():
-    places = np.arange(sources).reshape(ring_y, ring_z, cores)
-    return [[int(p) for p in places[:, z, :].reshape(-1)] for z in range(ring_z)]
+    return [[y * column + k for y in range(ring_y)] for k in range(column)]
 
 
 def line_groups():
@@ -83,7 +82,7 @@
     rows = [own_rows(own) for own in owns]
 
     def one(block, carry):
-        for far in range(ring_z):
+        for far in range(column):
             for node in range(len(owns)):
                 places, mass = read(node, block, far)
                 total[node] += pull_from(far_rows(places), rows[node], weight_rows(places, mass))
@@ -103,7 +102,7 @@
 
 def pulls(owns, read, total):
     total[...] = jnp.zeros_like(total)
-    add_pulls(owns, read, ring_y * cores, total)
+    add_pulls(owns, read, ring_y, total)
     return forces(owns, total)
 
 
@@ -122,7 +121,7 @@
     moved = [slice_length * (w[0] * speeds[0] + w[1] * speeds[1] + w[2] * speeds[2]) for w in lobatto_weights]
     first = places[0] + moved[0]
     packed = jnp.concatenate([*places, first, masses[...]], axis=0)
-    for k in range(ring_z):
+    for k in range(column):
         out[k] = packed
     known[0] = speeds[0]
     known[1] = first - half_step * speeds[1] + moved[1]
@@ -131,8 +130,8 @@
 
 def spread_kernel(far, out):
     for row in range(rows_sent):
-        line_of = jnp.concatenate([far[z, row : row + 1] for z in range(ring_z)], axis=0)
-        for k in range(ring_y * cores):
+        line_of = jnp.concatenate([far[z, row : row + 1] for z in range(column)], axis=0)
+        for k in range(ring_y):
             out[k, row] = line_of
 
 
@@ -146,7 +145,7 @@
 
 
 def near_block(here, block):
-    return (here[0] + block + 1) % (ring_y * cores)
+    return (here[0] + block + 1) % ring_y
 
 
 def column_kernel(far, own, total):
@@ -157,14 +156,14 @@
     add_pulls(nodes_of(own[0], 4), read, 1, total)
 
 
-def old_kernel(here, packed, own, known, column, out, state, total):
+def old_kernel(here, packed, own, known, begun, out, state, total):
     def read(node, block, far):
         near = near_block(here, block)
         return rows_of(packed, near, far, 3 * node)
 
-    total[...] = column[0:3]
+    total[...] = begun[0:3]
     owns = nodes_of(own[0], 3)
-    add_pulls(owns, read, ring_y * cores - 1, total)
+    add_pulls(owns, read, ring_y - 1, total)
     old = forces(owns, total)
     kicks = [slice_length * (w[0] * old[0] + w[1] * old[1] + w[2] * old[2]) for w in lobatto_weights]
     first_speed = known[0] + kicks[0]
@@ -180,15 +179,15 @@
     state[3] = second - known[2]
 
 
-def middle_kernel(here, now, packed, own, known, state, column, places, speeds, drift, total):
+def middle_kernel(here, now, packed, own, known, state, begun, places, speeds, drift, total):
     def read(node, block, far):
         near = near_block(here, block)
         return rows_of(packed, near, far, 9)
 
     mine = own[0]
-    total[...] = column[3:4]
+    total[...] = begun[3:4]
     owns = [mine[9:12]]
-    add_pulls(owns, read, ring_y * cores - 1, total)
+    add_pulls(owns, read, ring_y - 1, total)
     (force,) = forces(owns, total)
     last = state[1] + half_step * force
     for c in range(3):
@@ -213,7 +212,7 @@
 
 def end_kernel(packed, places, state, out, total):
     def read(node, near, far):
-        source = (near // cores) * (ring_z * cores) + far * cores + near % cores
+        source = near * column + far
         halves = [jnp.concatenate([places[source, c, h : h + 1] for c in range(3)], axis=0) for h in range(2)]
         return jnp.concatenate(halves, axis=1), packed[near, 12, far : far + 1]
 
@@ -269,20 +268,19 @@
     landing = [pltpu.VMEM(a.shape, f32) for a in (positions, velocities, masses)]
     own, known = run(
         pack_kernel,
-        (shape(ring_z, rows_sent, 256), shape(3, 3, 256)),
+        (shape(column, rows_sent, 256), shape(3, 3, 256)),
         places=(pltpu.HBM,) * 3,
         scratch=(*landing, pltpu.SemaphoreType.DMA((3,))),
         room=60,
     )(positions, velocities, masses)
     far = lax.all_to_all(own, "space", 0, 0, axis_index_groups=far_groups(), tiled=True)
-    near = run(spread_kernel, shape(ring_y * cores, rows_sent, ring_z, 256))(far)
+    near = run(spread_kernel, shape(ring_y, rows_sent, column, 256))(far)
     packed = lax.all_to_all(near, "space", 0, 0, axis_index_groups=near_groups(), tiled=True)
-    column = run(column_kernel, shape(4, 16, 256), flops=pull_flops)(far, own)
-    place = lax.axis_index("space").astype(jnp.int32)
-    place = ((place // (ring_z * cores)) * cores + place % cores)[None]
+    begun = run(column_kernel, shape(4, 16, 256), flops=pull_flops)(far, own)
+    place = (lax.axis_index("space").astype(jnp.int32) // column)[None]
     second, state = run(
         old_kernel, (shape(sources, 3, 2, 128), shape(4, 3, 256)), places=(pltpu.SMEM,), scratch=sums(3)
-    )(place, packed, own, known, column)
+    )(place, packed, own, known, begun)
     gathered = lax.all_to_all(second, "space", 0, 0, tiled=True)
     now = lax.axis_index("tm").astype(jnp.int32)[None]
     node_places, node_speeds, drift = run(
@@ -291,7 +289,7 @@
         places=(pltpu.SMEM, pltpu.SMEM),
         scratch=sums(1),
         flops=pull_flops,
-    )(place, now, packed, own, known, state, column)
+    )(place, now, packed, own, known, state, begun)
     others = [
         lax.ppermute(drift, "tm", [(t, t ^ (k * line)) for t in range(slices)]) for k in range(1, slices // line)
     ]

time: 83.6 us -> 84.2 us (level)
  waiting for transfers between devices: 12.6 us -> 9.58 us
  starting transfers between devices: 23.3 us -> 26.1 us
  blocking collectives: 28.1 us -> 29.5 us
    all_to_all x1, starting transfers between devices: 4.37 us -> 8.82 us  [body(): gathered = lax.all_to_all(second, 'space', 0, 0, tiled=True)]
    all_to_all x1, waiting for transfers between devices: 6.99 us -> 4.46 us  [body(): lax.all_to_all(near, 'space', 0, 0, axis_index_groups=near_groups(), tile...]
    all_to_all x1, starting transfers between devices: 6.19 us -> 4.31 us  [body(): lax.all_to_all(near, 'space', 0, 0, axis_index_groups=near_groups(), tile...]
    all_to_all x1, blocking collectives: 28.1 us -> 29.5 us  [body(): lax.all_to_all(own, 'space', 0, 0, axis_index_groups=far_groups(), tiled=...]
  transfers between devices with their start and end apart: 6 -> 6, of which waited for: 5 -> 5; matrix products, arithmetic and copies ran while one was open for 0% -> 0% of each run, Pallas kernels for 10% -> 11%
where the time goes in v6:
time: 84.2 us; the launch traced here: 83.6 us
  blocking collectives  29.5 us (35%)
  starting transfers between devices  26.1 us (31%)
  Pallas kernels  17.8 us (21%)
  waiting for transfers between devices  9.58 us (11%)
    all_to_all x1, blocking collectives, body(): lax.all_to_all(own, 'space', 0, 0, axis_index_groups=far_groups(), tiled=...  29.5 us
    pallas_call x8, Pallas kernels, call(): pl.pallas_call(kernel, in_specs=specs, out_shape=outs, scratch_shapes=lis...  17.8 us
    ppermute x3, starting transfers between devices, body(): lax.ppermute(drift, 'tm', [(t, t ^ k * line) for t in range(slices)])  8.97 us
    all_to_all x1, starting transfers between devices, body(): gathered = lax.all_to_all(second, 'space', 0, 0, tiled=True)  8.82 us
    all_to_all x1, waiting for transfers between devices, body(): lax.all_to_all(near, 'space', 0, 0, axis_index_groups=near_groups(), tile...  4.46 us
    all_to_all x1, starting transfers between devices, body(): lax.all_to_all(near, 'space', 0, 0, axis_index_groups=near_groups(), tile...  4.31 us
    all_to_all x1, starting transfers between devices, body(): lax.all_to_all(drift, 'tm', 0, 0, axis_index_groups=line_groups(), tiled=...  3.98 us
    ppermute x3, waiting for transfers between devices, body(): lax.ppermute(drift, 'tm', [(t, t ^ k * line) for t in range(slices)])  2.51 us
  transfers between devices with their start and end apart: 6, of which 5 were waited for; matrix products, arithmetic and copies ran while one was open for 0% of the time, Pallas kernels for 11%

profile of v6, /device:TPU:1, one launch (start us, length us, event | category | flops | bytes accessed | tf_op | source)
XLA Modules:
  0.0 83.6 jit_solution(12547892592149555267)
XLA Ops:
  0.6 1.4 %shard_map.92 = (f32[8,13,256]{2,1,0:T(8,128)}, f32[3,3,256]{2,1,0:T(4,128)}) custom-call(f32[3,3,1,256]{3,2,1,0:T(1,128)} %bitcast.10, f32[3,3,1,256]{3,2,1,0:T(1,128)} %bitcast.11, f32[1,256]{1,0:T(1,128)} %bitcast.12), custom_call_target="tpu_custom_call" | custom-call | tf_op jit(solution)/shard_map/pallas_call | solution.py:244
  2.1 29.5 %all_to_all.20.far = f32[8,13,256]{2,1,0:T(8,128)S(1)} all-to-all(f32[8,13,256]{2,1,0:T(8,128)} %get-tuple-element.16.own), channel_id=1, replica_groups={{0,1,2,3,4,5,6,7},{8,9,10,11,12,13,14,15},{16,17,18,19,20,21,22,23},{24..., dimensions={0} | all-to-all | bytes 212992 | tf_op jit(solution)/shard_map/all_to_all | solution.py:276
  31.5 0.8 shard_map.93
  32.3 0.0 copy-start
  32.3 4.3 %all-to-all-start.1 = ((f32[4,13,8,256]{3,2,1,0:T(8,128)}), f32[4,13,8,256]{3,2,1,0:T(8,128)S(1)}, u32[]{:S(2)}, u32[]{:S(2)}) async-start(f32[4,13,8,256]{3,2,1,0:T(8,128)} %shard_map.93), calls=%async_computation.1 | async-start | bytes 851968 | tf_op jit(solution)/shard_map/all_to_all | solution.py:278
  36.7 0.0 copy-done
  36.7 0.0 copy-start.1
  36.7 2.5 %shard_map.94.begun = f32[4,16,256]{2,1,0:T(8,128)S(1)} custom-call(f32[8,13,256]{2,1,0:T(8,128)S(1)} %all_to_all.20.far, f32[8,13,256]{2,1,0:T(8,128)S(1)} %copy-done), custom_call_target="tpu_custom_call" | custom-call | flops 3221225472 | tf_op jit(solution)/shard_map/pallas_call | solution.py:244
  39.2 4.5 %all-to-all-done.1.packed = f32[4,13,8,256]{3,2,1,0:T(8,128)S(1)} async-done(((f32[4,13,8,256]{3,2,1,0:T(8,128)}), f32[4,13,8,256]{3,2,1,0:T(8,128)S(1)}, u32[]{:S(2)}, u32[]{:S(2)}) %all-to-all-start.1) | async-done | bytes 426016 | tf_op jit(solution)/shard_map/all_to_all | solution.py:278
  43.7 0.0 copy-done.1
  43.7 6.0 %shard_map.95 = (f32[32,3,2,128]{3,2,1,0:T(2,128)}, f32[4,3,256]{2,1,0:T(4,128)S(1)}) custom-call(s32[1]{0:T(128)} %bitcast.here, f32[4,13,8,256]{3,2,1,0:T(8,128)S(1)} %all-to-all-done.1.packed, f32[8,13,256]{2,1,0:T(8,128)S(1)} %copy-done, f32[3,3,256]{2,1,0:T(4,128)S(1)} %copy-done.1, f32[4,16,256]{2,1,0:T(8,128)S(1)} %shard_map.94.begun), custom_call_target="tpu_custom_call" | custom-call | tf_op jit(solution)/shard_map/pallas_call | solution.py:244
  49.7 8.8 %all-to-all-start.2 = ((f32[32,3,2,128]{3,2,1,0:T(2,128)}), f32[32,3,2,128]{3,2,1,0:T(2,128)S(1)}, u32[]{:S(2)}, u32[]{:S(2)}) async-start(f32[32,3,2,128]{3,2,1,0:T(2,128)} %get-tuple-element.22), calls=%async_computation.2 | async-start | bytes 196608 | tf_op jit(solution)/shard_map/all_to_all | solution.py:284
  58.5 2.6 %shard_map.96 = (f32[1,3,2,256]{3,2,1,0:T(2,128)}, f32[1,3,2,256]{3,2,1,0:T(2,128)}, f32[6,256]{1,0:T(8,128)S(1)}) custom-call(s32[1]{0:T(128)} %bitcast.here, s32[1]{0:T(128)} %bitcast.1.now.here, f32[4,13,8,256]{3,2,1,0:T(8,128)S(1)} %all-to-all-done.1.packed, f32[8,13,256]{2,1,0:T(8,128)S(1)} %copy-done, f32[3,3,256]{2,1,0:T(4,128)S(1)} %copy-done.1, ...), custom_call_target="tpu_custom_call" | custom-call | flops 3221225472 | tf_op jit(solution)/shard_map/pallas_call | solution.py:244
  61.1 4.4 %collective-permute-start.2 = (f32[6,256]{1,0:T(8,128)S(1)}, f32[6,256]{1,0:T(8,128)S(1)}, u32[]{:S(2)}, u32[]{:S(2)}) collective-permute-start(f32[6,256]{1,0:T(8,128)S(1)} %get-tuple-element.21.drift), channel_id=1, source_target_pairs={{0,384},{32,416},{64,448},{96,480},{128,256},{160,288},{192,320},{... | collective-permute-start | bytes 18440 | tf_op jit(solution)/shard_map/ppermute | solution.py:294
  65.5 2.4 %collective-permute-start.1 = (f32[6,256]{1,0:T(8,128)S(1)}, f32[6,256]{1,0:T(8,128)S(1)}, u32[]{:S(2)}, u32[]{:S(2)}) collective-permute-start(f32[6,256]{1,0:T(8,128)S(1)} %get-tuple-element.21.drift), channel_id=1, source_target_pairs={{0,256},{32,288},{64,320},{96,352},{128,384},{160,416},{192,448},{... | collective-permute-start | bytes 18440 | tf_op jit(solution)/shard_map/ppermute | solution.py:294
  67.9 2.2 %collective-permute-start = (f32[6,256]{1,0:T(8,128)S(1)}, f32[6,256]{1,0:T(8,128)S(1)}, u32[]{:S(2)}, u32[]{:S(2)}) collective-permute-start(f32[6,256]{1,0:T(8,128)S(1)} %get-tuple-element.21.drift), channel_id=1, source_target_pairs={{0,128},{32,160},{64,192},{96,224},{128,0},{160,32},{192,64},{224,... | collective-permute-start | bytes 18440 | tf_op jit(solution)/shard_map/ppermute | solution.py:294
  70.1 0.0 collective-permute-done.2.others_and_out_2_
  70.1 1.6 %collective-permute-done.1.others_and_out_1_ = f32[6,256]{1,0:T(8,128)S(1)} collective-permute-done((f32[6,256]{1,0:T(8,128)S(1)}, f32[6,256]{1,0:T(8,128)S(1)}, u32[]{:S(2)}, u32[]{:S(2)}) %collective-permute-start.1) | collective-permute-done | bytes 6176 | tf_op jit(solution)/shard_map/ppermute | solution.py:294
  71.7 0.9 %collective-permute-done.others_and_out_0_ = f32[6,256]{1,0:T(8,128)S(1)} collective-permute-done((f32[6,256]{1,0:T(8,128)S(1)}, f32[6,256]{1,0:T(8,128)S(1)}, u32[]{:S(2)}, u32[]{:S(2)}) %collective-permute-start) | collective-permute-done | bytes 6176 | tf_op jit(solution)/shard_map/ppermute | solution.py:294
  72.6 0.6 shard_map.97
  73.3 1.1 %all-to-all-done.2.places = f32[32,3,2,128]{3,2,1,0:T(2,128)S(1)} async-done(((f32[32,3,2,128]{3,2,1,0:T(2,128)}), f32[32,3,2,128]{3,2,1,0:T(2,128)S(1)}, u32[]{:S(2)}, u32[]{:S(2)}) %all-to-all-start.2) | async-done | bytes 98336 | tf_op jit(solution)/shard_map/all_to_all | solution.py:284
  74.3 4.0 %all-to-all-start.3 = ((f32[4,12,256]{2,1,0:T(8,128)}), f32[4,12,256]{2,1,0:T(8,128)S(1)}, u32[]{:S(2)}, u32[]{:S(2)}) async-start(f32[4,12,256]{2,1,0:T(8,128)} %shard_map.97), calls=%async_computation.3 | async-start | bytes 131072 | tf_op jit(solution)/shard_map/all_to_all | solution.py:298
  78.3 0.0 copy-start.2
  78.3 0.0 copy-start.3
  78.3 3.1 %shard_map.98 = f32[3,1,256]{2,1,0:T(1,128)} custom-call(f32[4,13,8,256]{3,2,1,0:T(8,128)S(1)} %all-to-all-done.1.packed, f32[32,3,2,128]{3,2,1,0:T(2,128)S(1)} %all-to-all-done.2.places, f32[4,3,256]{2,1,0:T(4,128)S(1)} %get-tuple-element.18.state), custom_call_target="tpu_custom_call" | custom-call | flops 3221225472 | tf_op jit(solution)/shard_map/pallas_call | solution.py:244
  81.5 1.5 %all-to-all-done.3.drift = f32[4,12,256]{2,1,0:T(8,128)S(1)} async-done(((f32[4,12,256]{2,1,0:T(8,128)}), f32[4,12,256]{2,1,0:T(8,128)S(1)}, u32[]{:S(2)}, u32[]{:S(2)}) %all-to-all-start.3) | async-done | bytes 49184 | tf_op jit(solution)/shard_map/all_to_all | solution.py:298
  83.0 0.0 copy-done.2
  83.0 0.0 copy-done.3
  83.0 0.6 shard_map.99
Async XLA Ops:
  32.3 4.3 %copy-start = (f32[8,13,256]{2,1,0:T(8,128)S(1)}, f32[8,13,256]{2,1,0:T(8,128)}, u32[]{:S(2)}) copy-start(f32[8,13,256]{2,1,0:T(8,128)} %get-tuple-element.16.own) | copy-start | bytes 319492
  32.3 11.3 %all-to-all-start.1 = ((f32[4,13,8,256]{3,2,1,0:T(8,128)}), f32[4,13,8,256]{3,2,1,0:T(8,128)S(1)}, u32[]{:S(2)}, u32[]{:S(2)}) async-start(f32[4,13,8,256]{3,2,1,0:T(8,128)} %shard_map.93), calls=%async_computation.1 | async-start | bytes 851968 | tf_op jit(solution)/shard_map/all_to_all | solution.py:278
  36.7 7.0 %copy-start.1 = (f32[3,3,256]{2,1,0:T(4,128)S(1)}, f32[3,3,256]{2,1,0:T(4,128)}, u32[]{:S(2)}) copy-start(f32[3,3,256]{2,1,0:T(4,128)} %get-tuple-element.17.known) | copy-start | bytes 27652
  49.7 24.7 %all-to-all-start.2 = ((f32[32,3,2,128]{3,2,1,0:T(2,128)}), f32[32,3,2,128]{3,2,1,0:T(2,128)S(1)}, u32[]{:S(2)}, u32[]{:S(2)}) async-start(f32[32,3,2,128]{3,2,1,0:T(2,128)} %get-tuple-element.22), calls=%async_computation.2 | async-start | bytes 196608 | tf_op jit(solution)/shard_map/all_to_all | solution.py:284
  61.1 9.0 %collective-permute-start.2 = (f32[6,256]{1,0:T(8,128)S(1)}, f32[6,256]{1,0:T(8,128)S(1)}, u32[]{:S(2)}, u32[]{:S(2)}) collective-permute-start(f32[6,256]{1,0:T(8,128)S(1)} %get-tuple-element.21.drift), channel_id=1, source_target_pairs={{0,384},{32,416},{64,448},{96,480},{128,256},{160,288},{192,320},{... | collective-permute-start | bytes 18440 | tf_op jit(solution)/shard_map/ppermute | solution.py:294
  65.5 6.2 %collective-permute-start.1 = (f32[6,256]{1,0:T(8,128)S(1)}, f32[6,256]{1,0:T(8,128)S(1)}, u32[]{:S(2)}, u32[]{:S(2)}) collective-permute-start(f32[6,256]{1,0:T(8,128)S(1)} %get-tuple-element.21.drift), channel_id=1, source_target_pairs={{0,256},{32,288},{64,320},{96,352},{128,384},{160,416},{192,448},{... | collective-permute-start | bytes 18440 | tf_op jit(solution)/shard_map/ppermute | solution.py:294
  67.9 4.7 %collective-permute-start = (f32[6,256]{1,0:T(8,128)S(1)}, f32[6,256]{1,0:T(8,128)S(1)}, u32[]{:S(2)}, u32[]{:S(2)}) collective-permute-start(f32[6,256]{1,0:T(8,128)S(1)} %get-tuple-element.21.drift), channel_id=1, source_target_pairs={{0,128},{32,160},{64,192},{96,224},{128,0},{160,32},{192,64},{224,... | collective-permute-start | bytes 18440 | tf_op jit(solution)/shard_map/ppermute | solution.py:294
  74.3 8.7 %all-to-all-start.3 = ((f32[4,12,256]{2,1,0:T(8,128)}), f32[4,12,256]{2,1,0:T(8,128)S(1)}, u32[]{:S(2)}, u32[]{:S(2)}) async-start(f32[4,12,256]{2,1,0:T(8,128)} %shard_map.97), calls=%async_computation.3 | async-start | bytes 131072 | tf_op jit(solution)/shard_map/all_to_all | solution.py:298
  78.3 4.7 %copy-start.2 = (f32[3,256]{1,0:T(4,128)S(1)}, f32[3,256]{1,0:T(4,128)}, u32[]{:S(2)}) copy-start(f32[3,256]{1,0:T(4,128)} %places.1) | copy-start | bytes 9220
  78.3 4.7 %copy-start.3 = (f32[3,256]{1,0:T(4,128)S(1)}, f32[3,256]{1,0:T(4,128)}, u32[]{:S(2)}) copy-start(f32[3,256]{1,0:T(4,128)} %speeds.1) | copy-start | bytes 9220

commit v7 on v5

--- a/solution.py
+++ b/solution.py
@@ -129,11 +129,14 @@
     known[2] = places[0] + slice_length * speeds[0]
 
 
-def spread_kernel(far, out):
+def spread_kernel(far, out, once, sent):
     for row in range(rows_sent):
-        line_of = jnp.concatenate([far[z, row : row + 1] for z in range(ring_z)], axis=0)
-        for k in range(ring_y * cores):
-            out[k, row] = line_of
+        once[row] = jnp.concatenate([far[z, row : row + 1] for z in range(ring_z)], axis=0)
+    moves = [pltpu.make_async_copy(once, out.at[k], sent.at[k]) for k in range(ring_y * cores)]
+    for move in moves:
+        move.start()
+    for move in moves:
+        move.wait()
 
 
 def nodes_of(mine, count):
@@ -236,7 +239,7 @@
         start_speeds[c] = speed[c : c + 1]
 
 
-def run(kernel, outs, places=(), scratch=(), flops=0, room=40):
+def run(kernel, outs, places=(), scratch=(), flops=0, room=40, out_place=None):
     cost = pl.CostEstimate(flops=flops, bytes_accessed=0, transcendentals=0) if flops else None
 
     def call(*args):
@@ -246,6 +249,7 @@
             kernel,
             in_specs=specs,
             out_shape=outs,
+            **({"out_specs": pl.BlockSpec(memory_space=out_place)} if out_place else {}),
             scratch_shapes=list(scratch),
             cost_estimate=cost,
             compiler_params=pltpu.CompilerParams(vmem_limit_bytes=room * 2**20),
@@ -275,7 +279,12 @@
         room=60,
     )(positions, velocities, masses)
     far = lax.all_to_all(own, "space", 0, 0, axis_index_groups=far_groups(), tiled=True)
-    near = run(spread_kernel, shape(ring_y * cores, rows_sent, ring_z, 256))(far)
+    near = run(
+        spread_kernel,
+        shape(ring_y * cores, rows_sent, ring_z, 256),
+        scratch=(pltpu.VMEM((rows_sent, ring_z, 256), f32), pltpu.SemaphoreType.DMA((ring_y * cores,))),
+        out_place=pltpu.HBM,
+    )(far)
     packed = lax.all_to_all(near, "space", 0, 0, axis_index_groups=near_groups(), tiled=True)
     column = run(column_kernel, shape(4, 16, 256), flops=pull_flops)(far, own)
     place = lax.axis_index("space").astype(jnp.int32)

time: 83.6 us -> 83.7 us (level)
  no operation moved by 1% of the time
where the time goes in v7:
time: 83.7 us; the launch traced here: 82.5 us
  blocking collectives  28.1 us (34%)
  starting transfers between devices  23.3 us (28%)
  Pallas kernels  17.8 us (21%)
  waiting for transfers between devices  12.6 us (15%)
    all_to_all x1, blocking collectives, body(): lax.all_to_all(own, 'space', 0, 0, axis_index_groups=far_groups(), tiled=...  28.1 us
    pallas_call x8, Pallas kernels, call(): pl.pallas_call(kernel, in_specs=specs, out_shape=outs, **{'out_specs': pl...  17.8 us
    ppermute x3, starting transfers between devices, body(): lax.ppermute(drift, 'tm', [(t, t ^ k * line) for t in range(slices)])  8.97 us
    all_to_all x1, waiting for transfers between devices, body(): lax.all_to_all(near, 'space', 0, 0, axis_index_groups=near_groups(), tile...  6.98 us
    all_to_all x1, starting transfers between devices, body(): lax.all_to_all(near, 'space', 0, 0, axis_index_groups=near_groups(), tile...  6.2 us
    all_to_all x1, starting transfers between devices, body(): gathered = lax.all_to_all(second, 'space', 0, 0, tiled=True)  4.37 us
    all_to_all x1, starting transfers between devices, body(): lax.all_to_all(drift, 'tm', 0, 0, axis_index_groups=line_groups(), tiled=...  3.76 us
    ppermute x3, waiting for transfers between devices, body(): lax.ppermute(drift, 'tm', [(t, t ^ k * line) for t in range(slices)])  2.51 us
  transfers between devices with their start and end apart: 6, of which 5 were waited for; matrix products, arithmetic and copies ran while one was open for 0% of the time, Pallas kernels for 10%

profile of v7, /device:TPU:1, one launch (start us, length us, event | category | flops | bytes accessed | tf_op | source)
XLA Modules:
  0.0 82.5 jit_solution(5566823887615279948)
XLA Ops:
  0.6 1.4 %shard_map.92 = (f32[4,13,256]{2,1,0:T(8,128)}, f32[3,3,256]{2,1,0:T(4,128)}) custom-call(f32[3,3,1,256]{3,2,1,0:T(1,128)} %bitcast.10, f32[3,3,1,256]{3,2,1,0:T(1,128)} %bitcast.11, f32[1,256]{1,0:T(1,128)} %bitcast.12), custom_call_target="tpu_custom_call" | custom-call | tf_op jit(solution)/shard_map/pallas_call | solution.py:248
  2.0 28.1 %all_to_all.20.far = f32[4,13,256]{2,1,0:T(8,128)S(1)} all-to-all(f32[4,13,256]{2,1,0:T(8,128)} %get-tuple-element.16.own), channel_id=1, replica_groups={{0,2,4,6},{1,3,5,7},{8,10,12,14},{9,11,13,15},{16,18,20,22},{17,19,21,2..., dimensions={0} | all-to-all | bytes 106496 | tf_op jit(solution)/shard_map/all_to_all | solution.py:281
  30.2 0.9 %shard_map.93 = f32[8,13,4,256]{3,2,1,0:T(4,128)} custom-call(f32[4,13,256]{2,1,0:T(8,128)S(1)} %all_to_all.20.far), custom_call_target="tpu_custom_call" | custom-call | tf_op jit(solution)/shard_map/pallas_call | solution.py:248
  31.0 0.0 copy-start
  31.0 6.2 %all-to-all-start.1 = ((f32[8,13,4,256]{3,2,1,0:T(4,128)}), f32[8,13,4,256]{3,2,1,0:T(4,128)S(1)}, u32[]{:S(2)}, u32[]{:S(2)}) async-start(f32[8,13,4,256]{3,2,1,0:T(4,128)} %shard_map.93), calls=%async_computation.1 | async-start | bytes 851968 | tf_op jit(solution)/shard_map/all_to_all | solution.py:288
  37.2 0.0 copy-done
  37.2 0.0 copy-start.1
  37.2 1.4 %shard_map.94.column = f32[4,16,256]{2,1,0:T(8,128)S(1)} custom-call(f32[4,13,256]{2,1,0:T(8,128)S(1)} %all_to_all.20.far, f32[4,13,256]{2,1,0:T(8,128)S(1)} %copy-done), custom_call_target="tpu_custom_call" | custom-call | flops 3221225472 | tf_op jit(solution)/shard_map/pallas_call | solution.py:248
  38.7 7.0 %all-to-all-done.1.packed = f32[8,13,4,256]{3,2,1,0:T(4,128)S(1)} async-done(((f32[8,13,4,256]{3,2,1,0:T(4,128)}), f32[8,13,4,256]{3,2,1,0:T(4,128)S(1)}, u32[]{:S(2)}, u32[]{:S(2)}) %all-to-all-start.1) | async-done | bytes 426016 | tf_op jit(solution)/shard_map/all_to_all | solution.py:288
  45.7 0.0 copy-done.1
  45.7 6.8 %shard_map.95 = (f32[32,3,2,128]{3,2,1,0:T(2,128)}, f32[4,3,256]{2,1,0:T(4,128)S(1)}) custom-call(s32[1]{0:T(128)} %bitcast.here, f32[8,13,4,256]{3,2,1,0:T(4,128)S(1)} %all-to-all-done.1.packed, f32[4,13,256]{2,1,0:T(8,128)S(1)} %copy-done, f32[3,3,256]{2,1,0:T(4,128)S(1)} %copy-done.1, f32[4,16,256]{2,1,0:T(8,128)S(1)} %shard_map.94.column), custom_call_target="tpu_custom_call" | custom-call | tf_op jit(solution)/shard_map/pallas_call | solution.py:248
  52.5 4.4 %all-to-all-start.2 = ((f32[32,3,2,128]{3,2,1,0:T(2,128)}), f32[32,3,2,128]{3,2,1,0:T(2,128)S(1)}, u32[]{:S(2)}, u32[]{:S(2)}) async-start(f32[32,3,2,128]{3,2,1,0:T(2,128)} %get-tuple-element.22), calls=%async_computation.2 | async-start | bytes 196608 | tf_op jit(solution)/shard_map/all_to_all | solution.py:295
  56.9 2.9 %shard_map.96 = (f32[1,3,2,256]{3,2,1,0:T(2,128)}, f32[1,3,2,256]{3,2,1,0:T(2,128)}, f32[6,256]{1,0:T(8,128)S(1)}) custom-call(s32[1]{0:T(128)} %bitcast.here, s32[1]{0:T(128)} %bitcast.1.now.here, f32[8,13,4,256]{3,2,1,0:T(4,128)S(1)} %all-to-all-done.1.packed, f32[4,13,256]{2,1,0:T(8,128)S(1)} %copy-done, f32[3,3,256]{2,1,0:T(4,128)S(1)} %copy-done.1, ...), custom_call_target="tpu_custom_call" | custom-call | flops 3221225472 | tf_op jit(solution)/shard_map/pallas_call | solution.py:248
  59.8 4.4 %collective-permute-start.2 = (f32[6,256]{1,0:T(8,128)S(1)}, f32[6,256]{1,0:T(8,128)S(1)}, u32[]{:S(2)}, u32[]{:S(2)}) collective-permute-start(f32[6,256]{1,0:T(8,128)S(1)} %get-tuple-element.21.drift), channel_id=1, source_target_pairs={{0,384},{32,416},{64,448},{96,480},{128,256},{160,288},{192,320},{... | collective-permute-start | bytes 18440 | tf_op jit(solution)/shard_map/ppermute | solution.py:305
  64.2 2.4 %collective-permute-start.1 = (f32[6,256]{1,0:T(8,128)S(1)}, f32[6,256]{1,0:T(8,128)S(1)}, u32[]{:S(2)}, u32[]{:S(2)}) collective-permute-start(f32[6,256]{1,0:T(8,128)S(1)} %get-tuple-element.21.drift), channel_id=1, source_target_pairs={{0,256},{32,288},{64,320},{96,352},{128,384},{160,416},{192,448},{... | collective-permute-start | bytes 18440 | tf_op jit(solution)/shard_map/ppermute | solution.py:305
  66.6 2.2 %collective-permute-start = (f32[6,256]{1,0:T(8,128)S(1)}, f32[6,256]{1,0:T(8,128)S(1)}, u32[]{:S(2)}, u32[]{:S(2)}) collective-permute-start(f32[6,256]{1,0:T(8,128)S(1)} %get-tuple-element.21.drift), channel_id=1, source_target_pairs={{0,128},{32,160},{64,192},{96,224},{128,0},{160,32},{192,64},{224,... | collective-permute-start | bytes 18440 | tf_op jit(solution)/shard_map/ppermute | solution.py:305
  68.8 0.0 collective-permute-done.2.others_and_out_2_
  68.8 1.6 %collective-permute-done.1.others_and_out_1_ = f32[6,256]{1,0:T(8,128)S(1)} collective-permute-done((f32[6,256]{1,0:T(8,128)S(1)}, f32[6,256]{1,0:T(8,128)S(1)}, u32[]{:S(2)}, u32[]{:S(2)}) %collective-permute-start.1) | collective-permute-done | bytes 6176 | tf_op jit(solution)/shard_map/ppermute | solution.py:305
  70.4 0.9 %collective-permute-done.others_and_out_0_ = f32[6,256]{1,0:T(8,128)S(1)} collective-permute-done((f32[6,256]{1,0:T(8,128)S(1)}, f32[6,256]{1,0:T(8,128)S(1)}, u32[]{:S(2)}, u32[]{:S(2)}) %collective-permute-start) | collective-permute-done | bytes 6176 | tf_op jit(solution)/shard_map/ppermute | solution.py:305
  71.3 0.6 shard_map.97
  71.9 1.6 %all-to-all-done.2.places = f32[32,3,2,128]{3,2,1,0:T(2,128)S(1)} async-done(((f32[32,3,2,128]{3,2,1,0:T(2,128)}), f32[32,3,2,128]{3,2,1,0:T(2,128)S(1)}, u32[]{:S(2)}, u32[]{:S(2)}) %all-to-all-start.2) | async-done | bytes 98336 | tf_op jit(solution)/shard_map/all_to_all | solution.py:295
  73.6 3.8 %all-to-all-start.3 = ((f32[4,12,256]{2,1,0:T(8,128)}), f32[4,12,256]{2,1,0:T(8,128)S(1)}, u32[]{:S(2)}, u32[]{:S(2)}) async-start(f32[4,12,256]{2,1,0:T(8,128)} %shard_map.97), calls=%async_computation.3 | async-start | bytes 131072 | tf_op jit(solution)/shard_map/all_to_all | solution.py:309
  77.3 0.0 copy-start.2
  77.3 0.0 copy-start.3
  77.3 3.1 %shard_map.98 = f32[3,1,256]{2,1,0:T(1,128)} custom-call(f32[8,13,4,256]{3,2,1,0:T(4,128)S(1)} %all-to-all-done.1.packed, f32[32,3,2,128]{3,2,1,0:T(2,128)S(1)} %all-to-all-done.2.places, f32[4,3,256]{2,1,0:T(4,128)S(1)} %get-tuple-element.18.state), custom_call_target="tpu_custom_call" | custom-call | flops 3221225472 | tf_op jit(solution)/shard_map/pallas_call | solution.py:248
  80.5 1.4 %all-to-all-done.3.drift = f32[4,12,256]{2,1,0:T(8,128)S(1)} async-done(((f32[4,12,256]{2,1,0:T(8,128)}), f32[4,12,256]{2,1,0:T(8,128)S(1)}, u32[]{:S(2)}, u32[]{:S(2)}) %all-to-all-start.3) | async-done | bytes 49184 | tf_op jit(solution)/shard_map/all_to_all | solution.py:309
  81.9 0.0 copy-done.2
  81.9 0.0 copy-done.3
  81.9 0.6 shard_map.99
Async XLA Ops:
  31.0 6.2 %copy-start = (f32[4,13,256]{2,1,0:T(8,128)S(1)}, f32[4,13,256]{2,1,0:T(8,128)}, u32[]{:S(2)}) copy-start(f32[4,13,256]{2,1,0:T(8,128)} %get-tuple-element.16.own) | copy-start | bytes 159748
  31.0 14.6 %all-to-all-start.1 = ((f32[8,13,4,256]{3,2,1,0:T(4,128)}), f32[8,13,4,256]{3,2,1,0:T(4,128)S(1)}, u32[]{:S(2)}, u32[]{:S(2)}) async-start(f32[8,13,4,256]{3,2,1,0:T(4,128)} %shard_map.93), calls=%async_computation.1 | async-start | bytes 851968 | tf_op jit(solution)/shard_map/all_to_all | solution.py:288
  37.2 8.4 %copy-start.1 = (f32[3,3,256]{2,1,0:T(4,128)S(1)}, f32[3,3,256]{2,1,0:T(4,128)}, u32[]{:S(2)}) copy-start(f32[3,3,256]{2,1,0:T(4,128)} %get-tuple-element.17.known) | copy-start | bytes 27652
  52.5 21.1 %all-to-all-start.2 = ((f32[32,3,2,128]{3,2,1,0:T(2,128)}), f32[32,3,2,128]{3,2,1,0:T(2,128)S(1)}, u32[]{:S(2)}, u32[]{:S(2)}) async-start(f32[32,3,2,128]{3,2,1,0:T(2,128)} %get-tuple-element.22), calls=%async_computation.2 | async-start | bytes 196608 | tf_op jit(solution)/shard_map/all_to_all | solution.py:295
  59.8 9.0 %collective-permute-start.2 = (f32[6,256]{1,0:T(8,128)S(1)}, f32[6,256]{1,0:T(8,128)S(1)}, u32[]{:S(2)}, u32[]{:S(2)}) collective-permute-start(f32[6,256]{1,0:T(8,128)S(1)} %get-tuple-element.21.drift), channel_id=1, source_target_pairs={{0,384},{32,416},{64,448},{96,480},{128,256},{160,288},{192,320},{... | collective-permute-start | bytes 18440 | tf_op jit(solution)/shard_map/ppermute | solution.py:305
  64.2 6.2 %collective-permute-start.1 = (f32[6,256]{1,0:T(8,128)S(1)}, f32[6,256]{1,0:T(8,128)S(1)}, u32[]{:S(2)}, u32[]{:S(2)}) collective-permute-start(f32[6,256]{1,0:T(8,128)S(1)} %get-tuple-element.21.drift), channel_id=1, source_target_pairs={{0,256},{32,288},{64,320},{96,352},{128,384},{160,416},{192,448},{... | collective-permute-start | bytes 18440 | tf_op jit(solution)/shard_map/ppermute | solution.py:305
  66.6 4.7 %collective-permute-start = (f32[6,256]{1,0:T(8,128)S(1)}, f32[6,256]{1,0:T(8,128)S(1)}, u32[]{:S(2)}, u32[]{:S(2)}) collective-permute-start(f32[6,256]{1,0:T(8,128)S(1)} %get-tuple-element.21.drift), channel_id=1, source_target_pairs={{0,128},{32,160},{64,192},{96,224},{128,0},{160,32},{192,64},{224,... | collective-permute-start | bytes 18440 | tf_op jit(solution)/shard_map/ppermute | solution.py:305
  73.6 8.4 %all-to-all-start.3 = ((f32[4,12,256]{2,1,0:T(8,128)}), f32[4,12,256]{2,1,0:T(8,128)S(1)}, u32[]{:S(2)}, u32[]{:S(2)}) async-start(f32[4,12,256]{2,1,0:T(8,128)} %shard_map.97), calls=%async_computation.3 | async-start | bytes 131072 | tf_op jit(solution)/shard_map/all_to_all | solution.py:309
  77.3 4.6 %copy-start.2 = (f32[3,256]{1,0:T(4,128)S(1)}, f32[3,256]{1,0:T(4,128)}, u32[]{:S(2)}) copy-start(f32[3,256]{1,0:T(4,128)} %places.1) | copy-start | bytes 9220
  77.3 4.6 %copy-start.3 = (f32[3,256]{1,0:T(4,128)S(1)}, f32[3,256]{1,0:T(4,128)}, u32[]{:S(2)}) copy-start(f32[3,256]{1,0:T(4,128)} %speeds.1) | copy-start | bytes 9220
